TPU v7x, 128 devices: a whole 4x4x4 slice. The times are simulated.
128 devices in a mesh: qx: 8 (over z, core), qy: 16 (over y, x).
Axes of the slice: x: 4, y: 4, z: 4, core: 2. Of those that a mesh axis runs over, the one named last changes fastest.
Arguments:
- coeffs: float32 [8, 16, 8, 16, 2, 2, 16, 128], P('qx', 'qy'), may hold values from -0.75 to 0.75
- level_phase: float32 [8, 16, 8, 16, 4, 2, 128], P('qx', 'qy'), may hold values from -3.140625 to 3.140625
- field_phase: float32 [8, 16, 8, 16, 2, 128], P('qx', 'qy'), may hold values from -3.140625 to 3.140625
Outputs:
- field: float32 [8, 16, 8, 16, 2, 2, 16, 128], P('qx', 'qy')
All inputs are finite; a program needn't handle non-finite values.
Results may differ from a plain program's by a relative error of at most 0.0003.
Values sent between devices are 32-bit elements; how exact they have to be, the bound alone decides.
A program may use at most 128 MiB of HBM per device.

v0:
```python
import jax
import jax.numpy as jnp
import numpy as np
from jax import lax
from jax.sharding import PartitionSpec as P

CHEB = 8


def from_partner(value, axis, distance):
    mask = 2**distance
    pairs = [(source, source ^ mask) for source in range(lax.axis_size(axis))]
    return lax.ppermute(value, axis, pairs)


def point_tables(count):
    points = 0.5 - 0.5 * np.cos((2 * np.arange(count) + 1) * np.pi / (2 * count))

    def lagrange(places):
        values = np.ones((len(places), count))
        for k in range(count):
            for m in range(count):
                if m != k:
                    values[:, k] = values[:, k] * (places - points[m]) / (points[k] - points[m])
        return values

    halves = [lagrange((q + points) / 2.0) for q in range(2)]
    uniform = lagrange((np.arange(count) + 0.5) / count)
    identity = np.eye(2)
    children = np.stack(
        [
            np.stack(
                [
                    np.kron(identity, np.kron(halves[x_half], halves[y_half])).T
                    for y_half in range(2)
                ]
            )
            for x_half in range(2)
        ]
    )
    evaluate = np.kron(identity, np.kron(uniform, uniform)).T
    return (jnp.asarray(children, jnp.float32), jnp.asarray(evaluate, jnp.float32))


def rotate(values, angles):
    width = values.shape[-1] // 2
    cosine = jnp.cos(angles)
    sine = jnp.sin(angles)
    real_part = values[..., :width]
    imag_part = values[..., width:]
    return jnp.concatenate(
        [cosine * real_part - sine * imag_part, sine * real_part + cosine * imag_part], axis=-1
    )


def cross_x(values, bit):
    return from_partner(values, "qx", bit)


def cross_y(values, bit):
    return from_partner(values, "qy", bit)


def pair_level(state, angles, level, children):
    rotated = rotate(state, angles)
    y_bit = level - 1
    y_pick = lax.axis_index("qy") >> y_bit & 1
    if level == 1:
        partial_value = jnp.sum(rotated, axis=5, keepdims=True)
        total = partial_value + cross_y(partial_value, y_bit)
        chosen = lax.dynamic_index_in_dim(children, y_pick, 1, False)
        first = jnp.matmul(total, chosen[0], precision=lax.Precision.HIGHEST)
        second = jnp.matmul(total, chosen[1], precision=lax.Precision.HIGHEST)
        return jnp.concatenate([first, second], axis=5)
    x_bit = level - 2
    x_pick = lax.axis_index("qx") >> x_bit & 1
    partial_value = rotated + cross_x(rotated, x_bit)
    total = partial_value + cross_y(partial_value, y_bit)
    matrix = lax.dynamic_index_in_dim(
        lax.dynamic_index_in_dim(children, x_pick, 0, False), y_pick, 0, False
    )
    return jnp.matmul(total, matrix, precision=lax.Precision.HIGHEST)


def per_device(coeffs, level_phase, field_phase):
    children, evaluate = point_tables(CHEB)
    level_count = level_phase.shape[4]
    half_width = coeffs.shape[-1] // 2
    state = coeffs
    for level in range(1, level_count + 1):
        angles = level_phase[:, :, :, :, level - 1].reshape(
            level_phase.shape[:4] + (2, 2, 1, half_width)
        )
        state = pair_level(state, angles, level, children)
    values = jnp.matmul(state, evaluate, precision=lax.Precision.HIGHEST)
    angles = field_phase.reshape(field_phase.shape[:5] + (2, 1, half_width))
    return rotate(values, angles)


def solution(mesh):
    return jax.shard_map(
        per_device,
        mesh=mesh,
        in_specs=(
            P("qx", "qy", None, None, None, None, None, None),
            P("qx", "qy", None, None, None, None, None),
            P("qx", "qy", None, None, None, None),
        ),
        out_specs=P("qx", "qy", None, None, None, None, None, None),
        check_vma=False,
    )
```

profile of v0, /device:TPU:1, one launch (start us, length us, event | category | flops | bytes accessed | tf_op | source)
XLA Modules:
  0.0 580.6 jit_solution(1183396511252621472)
XLA Ops:
  0.0 8.2 %slice_cosine_fusion.3 = (f32[1,1,8,16,1,2,128]{6,5,4,3,2,1,0:T(2,128)S(1)}, f32[1,1,8,16,1,2,128]{6,5,4,3,2,1,0:T(2,128)S(1)}, f32[1,1,8,16,1,2,128]{6,5,4,3,2,...) fusion(f32[1,1,8,16,4,2,128]{6,5,4,3,2,1,0:T(2,128)} %param.6), kind=kLoop, calls=%fused_computation.44 | loop fusion | bytes 1572864 | tf_op jit(solution)/shard_map/cos | solution.py:47
  8.7 4.8 multiply_subtract_fusion.4
  13.5 1.4 maximum_reduce_fusion
  14.9 2.1 collective-permute-start
  17.8 44.2 %collective-permute-done = f32[1,1,8,16,2,1,16,128]{7,6,4,3,2,5,1,0:T(8,128)} collective-permute-done((f32[1,1,8,16,2,1,16,128]{7,6,4,3,2,5,1,0:T(8,128)S(1)}, f32[1,1,8,16,2,1,16,128]{7,6,4,3,2,5,1,0:T(8,128)}, u32[]{:S(2)}, u32[]{:S(2)}) %collective-permute-start) | collective-permute-done | bytes 2097184 | tf_op jit(solution)/shard_map/ppermute | solution.py:13
  62.0 3.4 fusion.18
  65.4 3.4 fusion.21
  68.9 1.9 multiply_subtract_fusion.3
  71.9 2.0 collective-permute-start.1
  73.9 6.8 %collective-permute-done.1 = f32[1,1,8,16,2,2,16,128]{7,6,4,3,2,5,1,0:T(8,128)S(1)} collective-permute-done((f32[1,1,8,16,2,2,16,128]{7,6,4,3,2,5,1,0:T(8,128)S(1)}, f32[1,1,8,16,2,2,16,128]{7,6,4,3,2,5,1,0:T(8,128)S(1)}, u32[]{:S(2)}, u32[]{:S(2)}) %collective-permute-start.1) | collective-permute-done | bytes 4194336 | tf_op jit(solution)/shard_map/ppermute | solution.py:13
  80.7 3.5 fusion.44
  84.2 3.0 collective-permute-start.2
  87.7 90.2 %collective-permute-done.2 = f32[1,1,8,16,2,2,16,128]{7,6,4,3,2,5,1,0:T(8,128)} collective-permute-done((f32[1,1,8,16,2,2,16,128]{7,6,4,3,2,5,1,0:T(8,128)}, f32[1,1,8,16,2,2,16,128]{7,6,4,3,2,5,1,0:T(8,128)}, u32[]{:S(2)}, u32[]{:S(2)}) %collective-permute-start.2) | collective-permute-done | bytes 4194336 | tf_op jit(solution)/shard_map/ppermute | solution.py:13
  177.9 5.9 %fusion.8 = f32[1,1,8,16,2,2,16,128]{7,6,5,4,3,2,1,0:T(8,128)S(1)} fusion(f32[2,2,128,128]{3,2,1,0:T(8,128)S(1)} %copy-done, s32[]{:T(128)S(6)} %select_n.38, s32[]{:T(128)S(6)} %select_n.40, f32[1,1,8,16,2,2,16,128]{7,6,4,3,2,5,1,0:T(8,128)} %fusion.44, f32[1,1,8,16,2,2,16,128]{7,6,4,3,2,5,1,0:T(8,128)} %collective-permute-done.2), kind=kOutput, calls=%fused_computation.26 | convolution fusion | flops 1611661312 | bytes 12648456 | tf_op jit(solution)/shard_map/dot_general | solution.py:82
  183.8 1.8 multiply_subtract_fusion.2
  185.6 1.2 pad_maximum_fusion.2
  186.8 1.9 collective-permute-start.3
  188.7 89.7 %collective-permute-done.3 = f32[1,1,8,16,2,2,16,128]{7,6,5,4,3,2,1,0:T(8,128)S(1)} collective-permute-done((f32[1,1,8,16,2,2,16,128]{7,6,5,4,3,2,1,0:T(8,128)S(1)}, f32[1,1,8,16,2,2,16,128]{7,6,5,4,3,2,1,0:T(8,128)S(1)}, u32[]{:S(2)}, u32[]{:S(2)}) %collective-permute-start.3) | collective-permute-done | bytes 4194336 | tf_op jit(solution)/shard_map/ppermute | solution.py:13
  278.4 3.5 fusion.43
  282.0 1.2 collective-permute-start.4
  283.6 88.9 %collective-permute-done.4 = f32[1,1,8,16,2,2,16,128]{7,6,5,4,3,2,1,0:T(8,128)} collective-permute-done((f32[1,1,8,16,2,2,16,128]{7,6,5,4,3,2,1,0:T(8,128)}, f32[1,1,8,16,2,2,16,128]{7,6,5,4,3,2,1,0:T(8,128)}, u32[]{:S(2)}, u32[]{:S(2)}) %collective-permute-start.4) | collective-permute-done | bytes 4194336 | tf_op jit(solution)/shard_map/ppermute | solution.py:13
  372.5 5.9 %fusion.11 = f32[1,1,8,16,2,2,16,128]{7,6,5,4,3,2,1,0:T(8,128)S(1)} fusion(f32[1,1,8,16,2,2,16,128]{7,6,5,4,3,2,1,0:T(8,128)} %fusion.43, f32[1,1,8,16,2,2,16,128]{7,6,5,4,3,2,1,0:T(8,128)} %collective-permute-done.4, f32[2,2,128,128]{3,2,1,0:T(8,128)S(1)} %copy-done, s32[]{:T(128)S(6)} %select_n.42, s32[]{:T(128)S(6)} %select_n.44), kind=kOutput, calls=%fused_computation.27 | convolution fusion | flops 1611661312 | bytes 12648456 | tf_op jit(solution)/shard_map/dot_general | solution.py:82
  378.4 1.8 multiply_subtract_fusion.1
  381.4 2.9 collective-permute-start.5
  384.3 88.0 %collective-permute-done.5 = f32[1,1,8,16,2,2,16,128]{7,6,5,4,3,2,1,0:T(8,128)S(1)} collective-permute-done((f32[1,1,8,16,2,2,16,128]{7,6,5,4,3,2,1,0:T(8,128)S(1)}, f32[1,1,8,16,2,2,16,128]{7,6,5,4,3,2,1,0:T(8,128)S(1)}, u32[]{:S(2)}, u32[]{:S(2)}) %collective-permute-start.5) | collective-permute-done | bytes 4194336 | tf_op jit(solution)/shard_map/ppermute | solution.py:13
  472.4 3.5 fusion.42
  475.9 2.7 collective-permute-start.6
  479.6 86.5 %collective-permute-done.6 = f32[1,1,8,16,2,2,16,128]{7,6,5,4,3,2,1,0:T(8,128)} collective-permute-done((f32[1,1,8,16,2,2,16,128]{7,6,5,4,3,2,1,0:T(8,128)}, f32[1,1,8,16,2,2,16,128]{7,6,5,4,3,2,1,0:T(8,128)}, u32[]{:S(2)}, u32[]{:S(2)}) %collective-permute-start.6) | collective-permute-done | bytes 4194336 | tf_op jit(solution)/shard_map/ppermute | solution.py:13
  566.1 6.0 %fusion = f32[8,16,2,2,16,128]{5,4,3,2,1,0:T(8,128)S(1)} fusion(f32[1,1,8,16,2,2,16,128]{7,6,5,4,3,2,1,0:T(8,128)} %fusion.42, f32[1,1,8,16,2,2,16,128]{7,6,5,4,3,2,1,0:T(8,128)} %collective-permute-done.6, f32[2,2,128,128]{3,2,1,0:T(8,128)S(1)} %copy-done, s32[]{:T(128)S(6)} %select_n.46, s32[]{:T(128)S(6)} %select_n.48), kind=kOutput, calls=%fused_computation.7 | convolution fusion | flops 1611661312 | bytes 12648456 | tf_op jit(solution)/shard_map/dot_general | solution.py:82
  572.2 3.6 convolution_bitcast_fusion
  575.8 1.7 multiply_subtract_fusion
  577.5 3.2 pad_maximum_fusion.4
  (21 shorter events, 5.5 us)
Async XLA Ops:
  14.9 47.1 %collective-permute-start = (f32[1,1,8,16,2,1,16,128]{7,6,4,3,2,5,1,0:T(8,128)S(1)}, f32[1,1,8,16,2,1,16,128]{7,6,4,3,2,5,1,0:T(8,128)}, u32[]{:S(2)}, u32[]{:S(2)}) collective-permute-start(f32[1,1,8,16,2,1,16,128]{7,6,4,3,2,5,1,0:T(8,128)S(1)} %bitcast.83), channel_id=1, source_target_pairs={{0,1},{1,0},{2,3},{3,2},{4,5},{5,4},{6,7},{7,6},{8,9},{9,8},{10,11... | collective-permute-start | bytes 6291464 | tf_op jit(solution)/shard_map/ppermute | solution.py:13
  71.9 106.0 %copy-start = (f32[2,2,128,128]{3,2,1,0:T(8,128)S(1)}, f32[2,2,128,128]{3,2,1,0:T(8,128)}, u32[]{:S(2)}) copy-start(f32[2,2,128,128]{3,2,1,0:T(8,128)} %constant.103.clone) | copy-start | bytes 786436
  71.9 8.8 %collective-permute-start.1 = (f32[1,1,8,16,2,2,16,128]{7,6,4,3,2,5,1,0:T(8,128)S(1)}, f32[1,1,8,16,2,2,16,128]{7,6,4,3,2,5,1,0:T(8,128)S(1)}, u32[]{:S(2)}, u32[]{:S(2)}) collective-permute-start(f32[1,1,8,16,2,2,16,128]{7,6,4,3,2,5,1,0:T(8,128)S(1)} %pad_maximum_fusion.1), channel_id=1, source_target_pairs={{0,16},{16,0},{32,48},{48,32},{64,80},{80,64},{96,112},{112,96},{1... | collective-permute-start | bytes 12582920 | tf_op jit(solution)/shard_map/ppermute | solution.py:13
  84.2 93.7 %collective-permute-start.2 = (f32[1,1,8,16,2,2,16,128]{7,6,4,3,2,5,1,0:T(8,128)}, f32[1,1,8,16,2,2,16,128]{7,6,4,3,2,5,1,0:T(8,128)}, u32[]{:S(2)}, u32[]{:S(2)}) collective-permute-start(f32[1,1,8,16,2,2,16,128]{7,6,4,3,2,5,1,0:T(8,128)} %fusion.44), channel_id=1, source_target_pairs={{0,2},{1,3},{2,0},{3,1},{4,6},{5,7},{6,4},{7,5},{8,10},{9,11},{10,... | collective-permute-start | bytes 12582920 | tf_op jit(solution)/shard_map/ppermute | solution.py:13
  186.8 91.6 %collective-permute-start.3 = (f32[1,1,8,16,2,2,16,128]{7,6,5,4,3,2,1,0:T(8,128)S(1)}, f32[1,1,8,16,2,2,16,128]{7,6,5,4,3,2,1,0:T(8,128)S(1)}, u32[]{:S(2)}, u32[]{:S(2)}) collective-permute-start(f32[1,1,8,16,2,2,16,128]{7,6,5,4,3,2,1,0:T(8,128)S(1)} %pad_maximum_fusion.2), channel_id=1, source_target_pairs={{0,32},{16,48},{32,0},{48,16},{64,96},{80,112},{96,64},{112,80},{1... | collective-permute-start | bytes 12582920 | tf_op jit(solution)/shard_map/ppermute | solution.py:13
  282.0 90.6 %collective-permute-start.4 = (f32[1,1,8,16,2,2,16,128]{7,6,5,4,3,2,1,0:T(8,128)}, f32[1,1,8,16,2,2,16,128]{7,6,5,4,3,2,1,0:T(8,128)}, u32[]{:S(2)}, u32[]{:S(2)}) collective-permute-start(f32[1,1,8,16,2,2,16,128]{7,6,5,4,3,2,1,0:T(8,128)} %fusion.43), channel_id=1, source_target_pairs={{0,4},{1,5},{2,6},{3,7},{4,0},{5,1},{6,2},{7,3},{8,12},{9,13},{10,... | collective-permute-start | bytes 12582920 | tf_op jit(solution)/shard_map/ppermute | solution.py:13
  381.4 97.1 %copy-start.1 = (f32[1,1,8,16,2,128]{5,4,3,2,1,0:T(2,128)S(1)}, f32[1,1,8,16,2,128]{5,4,3,2,1,0:T(2,128)}, u32[]{:S(2)}) copy-start(f32[1,1,8,16,2,128]{5,4,3,2,1,0:T(2,128)} %param.7) | copy-start | bytes 393220
  381.4 90.9 %collective-permute-start.5 = (f32[1,1,8,16,2,2,16,128]{7,6,5,4,3,2,1,0:T(8,128)S(1)}, f32[1,1,8,16,2,2,16,128]{7,6,5,4,3,2,1,0:T(8,128)S(1)}, u32[]{:S(2)}, u32[]{:S(2)}) collective-permute-start(f32[1,1,8,16,2,2,16,128]{7,6,5,4,3,2,1,0:T(8,128)S(1)} %pad_maximum_fusion.3), channel_id=1, source_target_pairs={{0,64},{16,80},{32,96},{48,112},{64,0},{80,16},{96,32},{112,48},{1... | collective-permute-start | bytes 12582920 | tf_op jit(solution)/shard_map/ppermute | solution.py:13
  475.9 90.2 %collective-permute-start.6 = (f32[1,1,8,16,2,2,16,128]{7,6,5,4,3,2,1,0:T(8,128)}, f32[1,1,8,16,2,2,16,128]{7,6,5,4,3,2,1,0:T(8,128)}, u32[]{:S(2)}, u32[]{:S(2)}) collective-permute-start(f32[1,1,8,16,2,2,16,128]{7,6,5,4,3,2,1,0:T(8,128)} %fusion.42), channel_id=1, source_target_pairs={{0,8},{1,9},{2,10},{3,11},{4,12},{5,13},{6,14},{7,15},{8,0},{9,1},... | collective-permute-start | bytes 12582920 | tf_op jit(solution)/shard_map/ppermute | solution.py:13
  479.5 92.6 %copy-start.2 = (f32[128,128,1,1,1,1]{1,0,5,4,3,2:T(8,128)S(1)}, f32[128,128,1,1,1,1]{1,0,5,4,3,2:T(8,128)}, u32[]{:S(2)}) copy-start(f32[128,128,1,1,1,1]{1,0,5,4,3,2:T(8,128)} %constant.108) | copy-start | bytes 196612
where the time goes:
time: 584 us; the launch traced here: 581 us
  waiting for transfers between devices  494 us (85%)
  other arithmetic  30.6 us (5%)
  matrix products  28.4 us (5%)
  starting transfers between devices  15.8 us (3%)
  local copies, waits for them, and re-layouts  11.4 us (2%)
    ppermute x7, waiting for transfers between devices, from_partner(): return lax.ppermute(value, axis, pairs)  494 us
    dot_general x3, matrix products, pair_level(): return jnp.matmul(total, matrix, precision=lax.Precision.HIGHEST)  17.9 us
    ppermute x7, starting transfers between devices, from_partner(): return lax.ppermute(value, axis, pairs)  15.8 us
    sub x5, other arithmetic, rotate(): cosine * real_part - sine * imag_part  12.1 us
  transfers between devices with their start and end apart: 7, of which 7 were waited for; matrix products, arithmetic and copies ran while one was open for 0% of the time, Pallas kernels for 0%

commit v1 on v0

v1 whole, which is shorter than its diff:
```python
import jax
import jax.numpy as jnp
import numpy as np
from jax import lax
from jax.sharding import PartitionSpec as P

CHEB = 8


def point_tables(count):
    points = 0.5 - 0.5 * np.cos((2 * np.arange(count) + 1) * np.pi / (2 * count))

    def lagrange(places):
        values = np.ones((len(places), count))
        for k in range(count):
            for m in range(count):
                if m != k:
                    values[:, k] = values[:, k] * (places - points[m]) / (points[k] - points[m])
        return values

    halves = [lagrange((q + points) / 2.0) for q in range(2)]
    uniform = lagrange((np.arange(count) + 0.5) / count)
    identity = np.eye(2)
    children = np.stack(
        [
            np.stack(
                [
                    np.kron(identity, np.kron(halves[x_half], halves[y_half])).T
                    for y_half in range(2)
                ]
            )
            for x_half in range(2)
        ]
    )
    evaluate = np.kron(identity, np.kron(uniform, uniform)).T
    return (jnp.asarray(children, jnp.float32), jnp.asarray(evaluate, jnp.float32))


def rotate(values, angles):
    width = values.shape[-1] // 2
    cosine = jnp.cos(angles)
    sine = jnp.sin(angles)
    real_part = values[..., :width]
    imag_part = values[..., width:]
    return jnp.concatenate(
        [cosine * real_part - sine * imag_part, sine * real_part + cosine * imag_part], axis=-1
    )


def spread(summed, x_axis, y_axis, children):
    stacked = []
    for x_half in range(2):
        columns = [
            jnp.matmul(summed, children[x_half, y_half], precision=lax.Precision.HIGHEST)
            for y_half in range(2)
        ]
        stacked.append(jnp.concatenate(columns, axis=y_axis))
    return jnp.concatenate(stacked, axis=x_axis)


def per_device(coeffs, level_phase, field_phase):
    children, evaluate = point_tables(CHEB)
    axes = ("qx", "qy")
    half = CHEB * CHEB
    boxes_h, boxes_v = coeffs.shape[2:4]
    rhs = coeffs.shape[6]
    n = boxes_h * boxes_v
    state = coeffs.reshape(n, 2, 2, rhs, 2 * half)
    phases = level_phase.reshape(n, 4, 2, 2, 1, half)
    partial = jnp.sum(rotate(state, phases[:, 0]), axis=2)
    moved_phase = lax.all_to_all(level_phase.reshape(n, 4, 2, 2 * half)[:, 1:], axes, 0, 0, tiled=True)
    moved = lax.all_to_all(partial, axes, 0, 0, tiled=True)
    digits = (2,) * 7
    summed = moved.reshape(digits + (1, 2, rhs, 2 * half)).sum(axis=6, keepdims=True)
    state = spread(summed, 7, 6, children)
    angles = moved_phase.reshape(digits + (3, 2, 2, half))
    for level in range(2, 5):
        turn = angles[:, :, :, :, :, :, :, level - 2]
        turn = jnp.swapaxes(turn, 7, 8).reshape(digits + (2, 2, 1, half))
        x_axis, y_axis = 4 - level, 7 - level
        summed = jnp.sum(rotate(state, turn), axis=(x_axis, y_axis), keepdims=True)
        if level < 4:
            state = spread(summed, x_axis, y_axis, children)
    out = jnp.broadcast_to(jnp.swapaxes(summed, 7, 8), digits + (2, 2, rhs, 2 * half))
    got = lax.all_to_all(out.reshape(n, 2, 2, rhs, 2 * half), axes, 0, 0, tiled=True)
    x_pick = lax.axis_index("qx") >> 2 & 1
    y_pick = lax.axis_index("qy") >> 3 & 1
    matrix = lax.dynamic_index_in_dim(
        lax.dynamic_index_in_dim(children, x_pick, 0, False), y_pick, 0, False
    )
    matrix = jnp.matmul(matrix, evaluate, precision=lax.Precision.HIGHEST)
    values = jnp.matmul(got, matrix, precision=lax.Precision.HIGHEST)
    values = rotate(values, field_phase.reshape(n, 2, 2, 1, half))
    return values.reshape(coeffs.shape)


def solution(mesh):
    return jax.shard_map(
        per_device,
        mesh=mesh,
        in_specs=(
            P("qx", "qy", None, None, None, None, None, None),
            P("qx", "qy", None, None, None, None, None),
            P("qx", "qy", None, None, None, None),
        ),
        out_specs=P("qx", "qy", None, None, None, None, None, None),
        check_vma=False,
    )
```

time: 584 us -> 167 us (0.29)
  waiting for transfers between devices: 494 us -> 65.4 us
  local copies, waits for them, and re-layouts: 11.4 us -> 30.5 us
  starting transfers between devices: 15.8 us -> 27 us
  other arithmetic: 30.6 us -> 22.1 us
  matrix products: 28.4 us -> 21.2 us
    ppermute x7 -> x0, waiting for transfers between devices: 494 us -> none  [from_partner(): return lax.ppermute(value, axis, pairs)]
    all_to_all x0 -> x3, waiting for transfers between devices: none -> 65.4 us  [the longest x1 49.2 us: per_device(): lax.all_to_all(out.reshape(n, 2, 2, rhs, 2 * half), axes, 0, 0, tiled=True)]
    all_to_all x0 -> x3, starting transfers between devices: none -> 27 us  [the longest x1 11.5 us: per_device(): lax.all_to_all(level_phase.reshape(n, 4, 2, 2 * half)[:, 1:], axes, 0, 0,...]
    ppermute x7 -> x0, starting transfers between devices: 15.8 us -> none  [from_partner(): return lax.ppermute(value, axis, pairs)]
    add x3 -> x0, other arithmetic: 10.6 us -> none  [pair_level(): partial_value = rotated + cross_x(rotated, x_bit)]
    dot_general x6 -> x14, matrix products: 28.4 us -> 21.2 us  [the longest x12 11.7 us: spread(): jnp.matmul(summed, children[x_half, y_half], precision=lax.Precision.HIGH...]
    cos x8, local copies, waits for them, and re-layouts: 10 us -> 16.2 us  [rotate(): cosine = jnp.cos(angles)]
  transfers between devices with their start and end apart: 7 -> 3, of which waited for: 7 -> 2; matrix products, arithmetic and copies ran while one was open for 0% -> 17% of each run, Pallas kernels for 0% -> 0%
where the time goes in v1:
time: 167 us
  waiting for transfers between devices  65.4 us (39%)
  local copies, waits for them, and re-layouts  30.5 us (18%)
  starting transfers between devices  27 us (16%)
  other arithmetic  22.1 us (13%)
  matrix products  21.2 us (13%)
    all_to_all x1, waiting for transfers between devices, per_device(): lax.all_to_all(out.reshape(n, 2, 2, rhs, 2 * half), axes, 0, 0, tiled=True)  49.2 us
    all_to_all x1, waiting for transfers between devices, per_device(): moved = lax.all_to_all(partial, axes, 0, 0, tiled=True)  16.2 us
    cos x8, local copies, waits for them, and re-layouts, rotate(): cosine = jnp.cos(angles)  16.2 us
    sub x5, other arithmetic, rotate(): cosine * real_part - sine * imag_part  11.7 us
    dot_general x12, matrix products, spread(): jnp.matmul(summed, children[x_half, y_half], precision=lax.Precision.HIGH...  11.7 us
    all_to_all x1, starting transfers between devices, per_device(): lax.all_to_all(level_phase.reshape(n, 4, 2, 2 * half)[:, 1:], axes, 0, 0,...  11.5 us
    all_to_all x1, starting transfers between devices, per_device(): moved = lax.all_to_all(partial, axes, 0, 0, tiled=True)  9.77 us
    dot_general x1, matrix products, per_device(): values = jnp.matmul(got, matrix, precision=lax.Precision.HIGHEST)  8.45 us
  transfers between devices with their start and end apart: 3, of which 2 were waited for; matrix products, arithmetic and copies ran while one was open for 17% of the time, Pallas kernels for 0%

profile of v1, /device:TPU:1, one launch (start us, length us, event | category | flops | bytes accessed | tf_op | source)
XLA Modules:
  0.0 166.7 jit_solution(12089206863812652089)
XLA Ops:
  0.0 1.8 %slice.84 = f32[128,3,2,128]{3,2,1,0:T(2,128)} slice(f32[128,4,2,128]{3,2,1,0:T(2,128)} %bitcast.114), slice={[0:128], [1:4], [0:2], [0:128]} | slice | bytes 786432 | tf_op jit(solution)/shard_map/slice | solution.py:71
  1.8 11.5 %all-to-all-start = ((f32[128,3,2,128]{3,2,1,0:T(2,128)}), f32[128,3,2,128]{3,2,1,0:T(2,128)S(1)}, u32[]{:S(2)}, u32[]{:S(2)}) async-start(f32[128,3,2,128]{3,2,1,0:T(2,128)} %slice.84), calls=%async_computation | async-start | bytes 786432 | tf_op jit(solution)/shard_map/all_to_all | solution.py:71
  13.3 1.1 copy.60
  15.1 3.7 %cosine_bitcast_fusion = (f32[128,2,2,64]{3,2,0,1:T(2,128)S(1)}, f32[128,2,2,64]{3,2,0,1:T(2,128)S(1)}) fusion(f32[128,4,2,2,1,64]{5,3,0,2,1,4:T(2,128)S(1)} %reshape.117), kind=kLoop, calls=%fused_computation.46 | loop fusion | bytes 393216 | tf_op jit(solution)/shard_map/cos | solution.py:41
  18.8 4.9 %multiply_subtract_fusion.3 = (f32[128,2,2,16,64]{4,3,2,1,0:T(8,128)S(1)}, f32[128,2,2,16,64]{4,3,2,1,0:T(8,128)S(1)}) fusion(f32[128,2,2,16,128]{4,3,2,1,0:T(8,128)} %bitcast.112, f32[128,2,2,64]{3,2,0,1:T(2,128)S(1)} %get-tuple-element.15, f32[128,2,2,64]{3,2,0,1:T(2,128)S(1)} %get-tuple-element.16), kind=kLoop, calls=%fused_computation.17 | loop fusion | flops 3145728 | bytes 8650752 | tf_op jit(solution)/shard_map/sub | solution.py:46
  23.8 2.7 %maximum_reduce_fusion = f32[128,2,16,128]{3,2,1,0:T(8,128)} fusion(f32[128,2,2,16,64]{4,3,2,1,0:T(8,128)S(1)} %get-tuple-element.12, f32[128,2,2,16,64]{4,3,2,1,0:T(8,128)S(1)} %get-tuple-element.11), kind=kLoop, calls=%fused_computation | loop fusion | flops 1572864 | bytes 6291456 | tf_op jit(solution)/shard_map/reduce_sum | solution.py:70
  26.5 9.8 %all-to-all-start.1 = ((f32[128,2,16,128]{3,2,1,0:T(8,128)}), f32[128,2,16,128]{3,2,1,0:T(8,128)S(1)}, u32[]{:S(2)}, u32[]{:S(2)}) async-start(f32[128,2,16,128]{3,2,1,0:T(8,128)} %maximum_reduce_fusion), calls=%async_computation.1 | async-start | bytes 4194304 | tf_op jit(solution)/shard_map/all_to_all | solution.py:72
  36.8 11.0 %cosine_bitcast_fusion.3 = (f32[2,2,2,2,2,2,2,2,2,64]{9,7,6,5,4,3,2,1,0,8:T(2,128)S(1)}, f32[2,2,2,2,2,2,2,2,2,64]{9,7,6,5,4,3,2,1,0,8:T(2,128)S(1)}, f32[2,2,2,...) fusion(f32[2,2,2,2,2,2,2,3,2,2,64]{10,9,6,5,4,3,2,1,0,8,7:T(2,1, ...), kind=kLoop, calls=%fused_computation.49 | loop fusion | bytes 1179648 | tf_op jit(solution)/shard_map/cos | solution.py:41
  49.7 16.2 %all-to-all-done.1 = f32[128,2,16,128]{3,2,1,0:T(8,128)S(1)} async-done(((f32[128,2,16,128]{3,2,1,0:T(8,128)}), f32[128,2,16,128]{3,2,1,0:T(8,128)S(1)}, u32[]{:S(2)}, u32[]{:S(2)}) %all-to-all-start.1) | async-done | bytes 2097184 | tf_op jit(solution)/shard_map/all_to_all | solution.py:72
  66.2 1.0 convolution_bitcast_fusion.10
  67.2 1.0 convolution_bitcast_fusion.11
  68.1 1.0 convolution_bitcast_fusion.8
  69.1 1.0 convolution_bitcast_fusion.9
  71.1 1.9 %multiply_subtract_fusion.2 = (f32[2,2,2,2,2,2,2,2,2,16,64]{10,9,8,5,4,3,2,1,0,7,6:T(8,128)S(1)}, f32[2,2,2,2,2,2,2,2,2,16,64]{10,9,8,5,4,3,2,1,0,7,6:T(8,128)S(1)}) fusion(f32[2,2,2,2,2,2,2,2,2,16,128]{10,9,8,5,4,3,2,1,0,7,6:T(8,128)S(1)} %maximum_maximum_fusion, f32[2,2,2,2,2,2,2,2,2,64]{9,8,5,4,3,2,1,0,7,6:T(2,128)S(1)} %copy-done, ...), kind=kLoop, calls=%fused_computation.15 | loop fusion | flops 3145728 | bytes 8650752 | tf_op jit(solution)/shard_map/sub | solution.py:46
  73.0 1.2 maximum_reduce_fusion.1
  75.2 1.0 convolution_bitcast_fusion.5
  76.1 1.0 convolution_bitcast_fusion.6
  77.1 1.0 convolution_bitcast_fusion.7
  78.6 1.7 %multiply_subtract_fusion.1 = (f32[2,2,2,2,2,2,2,2,2,16,64]{10,9,8,7,6,4,3,1,0,5,2:T(8,128)S(1)}, f32[2,2,2,2,2,2,2,2,2,16,64]{10,9,8,7,6,4,3,1,0,5,2:T(8,128)S(1)}) fusion(f32[2,2,2,2,2,2,2,2,2,16,128]{10,9,8,7,6,4,3,1,0,5,2:T(8,128)S(1)} %maximum_maximum_fusion.1, f32[2,2,2,2,2,2,2,2,2,64]{9,8,7,6,4,3,1,0,5,2:T(2,128)S(1)} %copy.68, ...), kind=kLoop, calls=%fused_computation.13 | loop fusion | flops 3145728 | bytes 8650752 | tf_op jit(solution)/shard_map/sub | solution.py:46
  80.3 1.2 maximum_reduce_fusion.2
  81.5 1.0 convolution_bitcast_fusion
  84.4 1.0 convolution_bitcast_fusion.3
  85.9 2.1 %multiply_subtract_fusion = (f32[2,2,2,2,2,2,2,2,2,16,64]{10,9,8,7,6,5,3,2,0,4,1:T(8,128)S(1)}, f32[2,2,2,2,2,2,2,2,2,16,64]{10,9,8,7,6,5,3,2,0,4,1:T(8,128)S(1)}) fusion(f32[2,2,2,2,2,2,2,2,2,16,128]{10,9,8,7,6,5,3,2,0,4,1:T(8,128)S(1)} %maximum_maximum_fusion.2, f32[2,2,2,2,2,2,2,2,2,64]{9,8,7,6,5,3,2,0,4,1:T(2,128)S(1)} %copy.73, ...), kind=kLoop, calls=%fused_computation.11 | loop fusion | flops 3145728 | bytes 8650752 | tf_op jit(solution)/shard_map/sub | solution.py:46
  88.1 1.2 maximum_reduce_fusion.3
  89.4 2.6 %broadcast_in_dim.15 = f32[2,2,2,2,2,2,2,2,2,16,128]{10,9,8,7,6,5,4,3,2,1,0:T(8,128)} broadcast(f32[2,2,2,2,2,2,2,16,128]{8,7,6,5,4,3,2,1,0:T(8,128)S(1)} %copy.74), dimensions={1,2,4,5,6,7,8,9,10} | broadcast | bytes 5242880 | tf_op jit(solution)/shard_map/broadcast_in_dim | solution.py:84
  91.9 5.7 %all-to-all-start.2 = ((f32[128,2,2,16,128]{4,3,2,1,0:T(8,128)}), f32[128,2,2,16,128]{4,3,2,1,0:T(8,128)}, u32[]{:S(2)}, u32[]{:S(2)}) async-start(f32[128,2,2,16,128]{4,3,2,1,0:T(8,128)} %bitcast.111), calls=%async_computation.2 | async-start | bytes 8388608 | tf_op jit(solution)/shard_map/all_to_all | solution.py:85
  99.0 1.1 convolution_bitcast_fusion.12
  100.1 49.2 %all-to-all-done.2 = f32[128,2,2,16,128]{4,3,2,1,0:T(8,128)} async-done(((f32[128,2,2,16,128]{4,3,2,1,0:T(8,128)}), f32[128,2,2,16,128]{4,3,2,1,0:T(8,128)}, u32[]{:S(2)}, u32[]{:S(2)}) %all-to-all-start.2) | async-done | bytes 4194336 | tf_op jit(solution)/shard_map/all_to_all | solution.py:85
  149.3 8.4 %fusion = f32[128,2,2,16,128]{0,4,3,2,1:T(8,128)S(1)} fusion(f32[128,128,1,1,1]{0,1,4,3,2:T(8,128)S(1)} %convolution_bitcast_fusion.12, f32[128,2,2,16,128]{4,3,2,1,0:T(8,128)} %all-to-all-done.2), kind=kOutput, calls=%fused_computation.8 | convolution fusion | flops 1610612736 | bytes 8454144 | tf_op jit(solution)/shard_map/dot_general | solution.py:92
  157.8 1.0 multiply_subtract_fusion.4
  158.8 2.4 %pad_maximum_fusion = f32[128,2,2,16,128]{0,4,3,2,1:T(8,128)} fusion(f32[128,2,2,16,64]{0,4,3,2,1:T(8,128)S(1)} %get-tuple-element.14, f32[128,2,2,16,64]{0,4,3,2,1:T(8,128)S(1)} %get-tuple-element.13), kind=kLoop, calls=%fused_computation.7 | loop fusion | flops 1048576 | bytes 8388608 | tf_op jit(solution)/shard_map/concatenate | solution.py:45
  161.2 5.4 %copy.79 = f32[128,2,2,16,128]{4,3,2,1,0:T(8,128)} copy(f32[128,2,2,16,128]{0,4,3,2,1:T(8,128)} %pad_maximum_fusion) | data formatting | bytes 8388608 | tf_op jit(solution)/shard_map/concatenate | solution.py:45
  (37 shorter events, 9.5 us)
Async XLA Ops:
  1.8 24.6 %all-to-all-start = ((f32[128,3,2,128]{3,2,1,0:T(2,128)}), f32[128,3,2,128]{3,2,1,0:T(2,128)S(1)}, u32[]{:S(2)}, u32[]{:S(2)}) async-start(f32[128,3,2,128]{3,2,1,0:T(2,128)} %slice.84), calls=%async_computation | async-start | bytes 786432 | tf_op jit(solution)/shard_map/all_to_all | solution.py:71
  26.5 39.5 %all-to-all-start.1 = ((f32[128,2,16,128]{3,2,1,0:T(8,128)}), f32[128,2,16,128]{3,2,1,0:T(8,128)S(1)}, u32[]{:S(2)}, u32[]{:S(2)}) async-start(f32[128,2,16,128]{3,2,1,0:T(8,128)} %maximum_reduce_fusion), calls=%async_computation.1 | async-start | bytes 4194304 | tf_op jit(solution)/shard_map/all_to_all | solution.py:72
  36.7 29.4 %copy-start.1 = (f32[128,128,1,1,1,1,1,1,1]{1,0,8,7,6,5,4,3,2:T(8,128)S(1)}, f32[128,128,1,1,1,1,1,1,1]{1,0,8,7,6,5,4,3,2:T(8,128)}, u32[]{:S(2)}) copy-start(f32[128,128,1,1,1,1,1,1,1]{1,0,8,7,6,5,4,3,2:T(8,128)} %constant.64) | copy-start | bytes 196612
  47.8 19.4 %copy-start.2 = (f32[128,128,1,1,1,1,1,1,1]{1,0,8,7,6,5,4,3,2:T(8,128)S(1)}, f32[128,128,1,1,1,1,1,1,1]{1,0,8,7,6,5,4,3,2:T(8,128)}, u32[]{:S(2)}) copy-start(f32[128,128,1,1,1,1,1,1,1]{1,0,8,7,6,5,4,3,2:T(8,128)} %constant.63) | copy-start | bytes 196612
  65.9 2.2 %copy-start.4 = (f32[128,128,1,1,1,1,1,1,1]{1,0,8,7,6,5,4,3,2:T(8,128)S(1)}, f32[128,128,1,1,1,1,1,1,1]{1,0,8,7,6,5,4,3,2:T(8,128)}, u32[]{:S(2)}) copy-start(f32[128,128,1,1,1,1,1,1,1]{1,0,8,7,6,5,4,3,2:T(8,128)} %constant.66) | copy-start | bytes 196612
  65.9 3.2 %copy-start.3 = (f32[128,128,1,1,1,1,1,1,1]{1,0,8,7,6,5,4,3,2:T(8,128)S(1)}, f32[128,128,1,1,1,1,1,1,1]{1,0,8,7,6,5,4,3,2:T(8,128)}, u32[]{:S(2)}) copy-start(f32[128,128,1,1,1,1,1,1,1]{1,0,8,7,6,5,4,3,2:T(8,128)} %constant.65) | copy-start | bytes 196612
  70.1 1.0 copy-start
  91.9 5.8 %copy-start.5 = (f32[1,1,8,16,2,128]{5,4,3,2,1,0:T(2,128)S(1)}, f32[1,1,8,16,2,128]{5,4,3,2,1,0:T(2,128)}, u32[]{:S(2)}) copy-start(f32[1,1,8,16,2,128]{5,4,3,2,1,0:T(2,128)} %param.7) | copy-start | bytes 393220
  91.9 7.1 %copy-start.6 = (f32[128,128]{1,0:T(8,128)S(1)}, f32[128,128]{1,0:T(8,128)}, u32[]{:S(2)}) copy-start(f32[128,128]{1,0:T(8,128)} %constant.51.clone) | copy-start | bytes 196612
  91.9 57.4 %all-to-all-start.2 = ((f32[128,2,2,16,128]{4,3,2,1,0:T(8,128)}), f32[128,2,2,16,128]{4,3,2,1,0:T(8,128)}, u32[]{:S(2)}, u32[]{:S(2)}) async-start(f32[128,2,2,16,128]{4,3,2,1,0:T(8,128)} %bitcast.111), calls=%async_computation.2 | async-start | bytes 8388608 | tf_op jit(solution)/shard_map/all_to_all | solution.py:85

commit v2 on v0

v2 whole, which is shorter than its diff:
```python
import functools

import jax
import jax.numpy as jnp
import numpy as np
from jax import lax
from jax.experimental import pallas as pl
from jax.experimental.pallas import tpu as pltpu
from jax.sharding import PartitionSpec as P

CHEB = 8
PTS = CHEB * CHEB
WIDE = 2 * PTS
MESH = pl.DeviceIdType.MESH
F32 = jnp.float32
BF16 = jnp.bfloat16


def point_tables(count):
    points = 0.5 - 0.5 * np.cos((2 * np.arange(count) + 1) * np.pi / (2 * count))

    def lagrange(places):
        values = np.ones((len(places), count))
        for k in range(count):
            for m in range(count):
                if m != k:
                    values[:, k] = values[:, k] * (places - points[m]) / (points[k] - points[m])
        return values

    halves = [lagrange((q + points) / 2.0) for q in range(2)]
    uniform = lagrange((np.arange(count) + 0.5) / count)
    identity = np.eye(2)
    children = [
        [np.kron(identity, np.kron(halves[q], halves[s])).T for s in range(2)] for q in range(2)
    ]
    evaluate = np.kron(identity, np.kron(uniform, uniform)).T
    return children, evaluate


def three_parts(matrix):
    high = matrix.astype(np.float32).astype(BF16)
    low = (matrix - high.astype(np.float64)).astype(np.float32).astype(BF16)
    return np.concatenate([high, high, low], axis=0)


def weights():
    children, evaluate = point_tables(CHEB)
    spread = three_parts(np.concatenate([children[q][s] for q in range(2) for s in range(2)], axis=1))
    last = []
    for q in range(2):
        for s in range(2):
            both = children[q][s] @ evaluate
            swapped = np.concatenate([both[:, PTS:], both[:, :PTS]], axis=1)
            last.append(three_parts(np.concatenate([both, swapped], axis=1)))
    return jnp.asarray(spread), jnp.asarray(np.stack(last))


def split_parts(value):
    high = value.astype(BF16)
    low = (value - high.astype(F32)).astype(BF16)
    return high, low


def sine_cosine(angle):
    u = angle * 0.5
    w = u * u
    s = -2.5052108e-08
    for c in (2.7557319e-06, -1.9841270e-04, 8.3333333e-03, -1.6666667e-01, 1.0):
        s = s * w + c
    s = s * u
    c_ = 2.0876757e-09
    for c in (-2.7557319e-07, 2.4801587e-05, -1.3888889e-03, 4.1666667e-02, -0.5, 1.0):
        c_ = c_ * w + c
    return 2.0 * s * c_, 1.0 - 2.0 * s * s


def swap(value):
    return pltpu.roll(value, PTS, value.ndim - 1)


def turn_tables(angle, before):
    sine, cosine = sine_cosine(angle)
    lane = lax.broadcasted_iota(jnp.int32, angle.shape, angle.ndim - 1)
    low = lane < PTS
    cos_swap, sin_swap = swap(cosine), swap(sine)
    cos = (jnp.where(low, cosine, cos_swap), jnp.where(low, cos_swap, cosine))
    if before:
        sin = (jnp.where(low, sine, -sin_swap), jnp.where(low, sin_swap, -sine))
    else:
        sin = (jnp.where(low, -sine, sin_swap), jnp.where(low, -sin_swap, sine))
    return cos, sin


def wait_for(ref, sem):
    pltpu.make_async_copy(ref, ref, sem).wait()


def exchange_kernel(
    coeffs, phases, w_ref, gz, gy,
    cbuf, lpv, cos1, sin1, sendx, recvx, send1, recv1, p1, phs, cos_t, sin_t, xs, res, s4, r1,
    load_sem, x_send, x_recv, in_send, in_recv, s1_send, s1_recv, s2_send, s2_recv, own_sem,
    ph_send, ph_recv,
):
    big_x = lax.axis_index("qx")
    big_y = lax.axis_index("qy")
    z, core = big_x // 2, big_x % 2
    y, x = big_y // 4, big_y % 4

    phase_load = pltpu.make_async_copy(phases, lpv, load_sem.at[2])
    phase_load.start()
    loads = []
    for left in range(2):
        load = pltpu.make_async_copy(coeffs.at[:, left], cbuf.at[left], load_sem.at[left])
        load.start()
        loads.append(load)

    def device(dz, dc, dy, dx):
        return ((z + dz) % 4) * 2 + (core + dc) % 2, ((y + dy) % 4) * 4 + (x + dx) % 4

    barrier = pltpu.get_barrier_semaphore()
    greeted = 0
    for dz in range(4):
        for dc in range(2):
            for dy in range(4):
                for dx in range(4):
                    if (dz, dc, dy, dx) != (0, 0, 0, 0) and 0 in (dz, dy, dx):
                        pl.semaphore_signal(
                            barrier, inc=1, device_id=device(dz, dc, dy, dx), device_id_type=MESH
                        )
                        greeted += 1

    def send(src, dst, send_sem, recv_sem, target):
        pltpu.make_async_remote_copy(
            src_ref=src, dst_ref=dst, send_sem=send_sem, recv_sem=recv_sem,
            device_id=target, device_id_type=MESH,
        ).start()

    phase_load.wait()

    def first_tables(i, carry):
        cos, sin = turn_tables(lpv[i], True)
        for k in range(2):
            cos1[k, i] = cos[k]
            sin1[k, i] = sin[k]
        return carry

    lax.fori_loop(0, 128, first_tables, 0)

    def rotate_first(c):
        left, half = c // 2, c % 2
        if half == 0:
            loads[left].wait()

        def step(i, carry):
            for vx in range(4):
                box = i * 4 + vx
                direct = None
                crossed = None
                for k in range(2):
                    value = cbuf[left, box, k, pl.ds(half * 8, 8), :]
                    d = value * cos1[k, box, pl.ds(left, 1), :]
                    e = value * sin1[k, box, pl.ds(left, 1), :]
                    direct = d if direct is None else direct + d
                    crossed = e if crossed is None else crossed + e
                sendx[c, vx, i] = direct + swap(crossed)
            return carry

        lax.fori_loop(0, 32, step, 0)

    def send_x(c):
        for dx in range(1, 4):
            there = (x + dx) % 4
            send(sendx.at[c, there], recvx.at[c, x], x_send.at[c], x_recv.at[c], (big_x, y * 4 + there))

    rotate_first(0)
    pl.semaphore_wait(barrier, greeted)
    send_x(0)

    me_in = big_x * 4 + y

    def send_phase(d, carry):
        there_x = ((z + d // 8) % 4) * 2 + (core + (d // 4) % 2) % 2
        there_y = (y + d % 4) % 4
        send(
            lpv.at[pl.ds((there_x * 4 + there_y) * 4, 4)], p1.at[me_in], ph_send.at[0], ph_recv.at[0],
            (there_x, there_y * 4 + x),
        )
        return carry

    lax.fori_loop(1, 32, send_phase, 0)
    for vx in range(4):
        p1[me_in, vx] = lpv[me_in * 4 + vx]

    for c in range(1, 4):
        rotate_first(c)
        if c == 1:
            wait_for(p1.at[pl.ds(0, 31)], ph_recv.at[0])
            for dx in range(1, 4):
                there = (x + dx) % 4
                send(p1.at[:, there], phs.at[:, x], ph_send.at[1], ph_recv.at[1], (big_x, y * 4 + there))
        send_x(c)

    def pass_on(c):
        wait_for(recvx.at[c, pl.ds(0, 3)], x_recv.at[c])

        def own(i, carry):
            recvx[c, x, i] = sendx[c, x, i]
            return carry

        lax.fori_loop(0, 32, own, 0)

        def add(i, carry):
            for y1 in range(2):
                send1[c, i, y1] = recvx[c, 2 * y1, i] + recvx[c, 2 * y1 + 1, i]
            return carry

        lax.fori_loop(0, 32, add, 0)

        def push(d, carry):
            there_x = ((z + d // 8) % 4) * 2 + (core + (d // 4) % 2) % 2
            there_y = (y + d % 4) % 4
            send(
                send1.at[c, there_x * 4 + there_y], recv1.at[c, me_in], in_send.at[c], in_recv.at[c],
                (there_x, there_y * 4 + x),
            )
            return carry

        lax.fori_loop(1, 32, push, 0)
        for y1 in range(2):
            recv1[c, me_in, y1] = send1[c, me_in, y1]

    def put_parts(row, value):
        high, low = split_parts(value)
        rows = pl.ds(pl.multiple_of(row, 16), 16)
        xs[rows, 0:WIDE] = high
        xs[rows, WIDE : 2 * WIDE] = low
        xs[rows, 2 * WIDE : 3 * WIDE] = high

    def multiply():
        def piece(i, carry):
            rows = pl.ds(pl.multiple_of(i * 256, 256), 256)
            res[rows, :] = jnp.dot(xs[rows, :], w_ref[...], preferred_element_type=F32)
            return carry

        lax.fori_loop(0, 2, piece, 0)

    def turned_sum(parts, row):
        direct = None
        crossed = None
        for block, column, k, place in parts:
            value = res[pl.ds(pl.multiple_of(block * 8, 8), 8), column * WIDE : (column + 1) * WIDE]
            d = value * cos_t[k, place, pl.ds(row, 1), :]
            e = value * sin_t[k, place, pl.ds(row, 1), :]
            direct = d if direct is None else direct + d
            crossed = e if crossed is None else crossed + e
        return direct + swap(crossed)

    def levels(c):
        left, half = c // 2, c % 2
        wait_for(recv1.at[c, pl.ds(0, 31)], in_recv.at[c])

        def first(i, carry):
            put_parts(i * 16, recv1[c, i].reshape(16, WIDE))
            return carry

        lax.fori_loop(0, 32, first, 0)
        multiply()
        if c == 0:
            phase_tables()

        def second(t, carry):
            x2, x1, y3, y2 = t // 8, (t // 4) % 2, (t // 2) % 2, t % 2
            for y0 in range(2):
                outs = []
                for k in range(2):
                    parts = []
                    for x0 in range(2):
                        for y1 in range(2):
                            block = x2 * 32 + x1 * 16 + x0 * 8 + y3 * 4 + y2 * 2 + y1
                            place = (x2 * 4 + x1 * 2 + x0) * 16 + y3 * 8 + y2 * 4 + y1 * 2 + y0
                            parts.append((block, k * 2 + y0, k, place))
                    outs.append(turned_sum(parts, 2 + left))
                put_parts((t * 2 + y0) * 16, jnp.concatenate(outs, axis=0))
            return carry

        lax.fori_loop(0, 16, second, 0)
        multiply()

        def third(t, carry):
            x2, y3, y0, k = t // 8, (t // 4) % 2, (t // 2) % 2, t % 2
            for x0 in range(2):
                outs = []
                for y1 in range(2):
                    parts = []
                    for x1 in range(2):
                        for y2 in range(2):
                            block = x2 * 32 + x1 * 16 + y3 * 8 + y2 * 4 + y0 * 2 + k
                            place = (x2 * 4 + x1 * 2 + x0) * 16 + y3 * 8 + y2 * 4 + y1 * 2 + y0
                            parts.append((block, x0 * 2 + y1, k, place))
                    outs.append(turned_sum(parts, 4 + left))
                put_parts((t * 2 + x0) * 16, jnp.concatenate(outs, axis=0))
            return carry

        lax.fori_loop(0, 16, third, 0)
        multiply()

        def fourth(t, carry):
            y0, k, x0, y1 = t // 8, (t // 4) % 2, (t // 2) % 2, t % 2
            for x1 in range(2):
                for y2 in range(2):
                    parts = []
                    for x2 in range(2):
                        for y3 in range(2):
                            block = x2 * 32 + y3 * 16 + y0 * 8 + k * 4 + x0 * 2 + y1
                            place = (x2 * 4 + x1 * 2 + x0) * 16 + y3 * 8 + y2 * 4 + y1 * 2 + y0
                            parts.append((block, x1 * 2 + y2, k, place))
                    if half == 0:
                        s4[c, x0 * 8 + y2 * 4 + y1 * 2 + y0, x1, k] = turned_sum(parts, 6 + left)
                    else:
                        s4[c, x1 * 8 + x0 * 4 + y1 * 2 + y0, y2, k] = turned_sum(parts, 6 + left)
            return carry

        lax.fori_loop(0, 16, fourth, 0)

    def phase_tables():
        wait_for(phs.at[:, pl.ds(0, 3)], ph_recv.at[1])

        def own(i, carry):
            phs[i, x] = p1[i, x]
            return carry

        lax.fori_loop(0, 32, own, 0)

        def table(i, carry):
            for sx in range(4):
                cos, sin = turn_tables(phs[i, sx], True)
                for k in range(2):
                    cos_t[k, i * 4 + sx] = cos[k]
                    sin_t[k, i * 4 + sx] = sin[k]
            return carry

        lax.fori_loop(0, 32, table, 0)

    def out_first(c):
        half = c % 2
        if half == 0:
            me = core * 16 + y * 4 + x

            def push(d, carry):
                there_c = (core + d // 16) % 2
                there_y = (y + (d // 4) % 4) % 4
                there_x = (x + d % 4) % 4
                send(
                    s4.at[c, there_c * 8 + (there_y % 2) * 4 + there_x], r1.at[c, me],
                    s1_send.at[c], s1_recv.at[c], (z * 2 + there_c, there_y * 4 + there_x),
                )
                return carry

            mine = core * 8 + (y % 2) * 4 + x
        else:
            me = (z * 2 + core) * 4 + x

            def push(d, carry):
                there_c = (core + d // 16) % 2
                there_z = (z + (d // 4) % 4) % 4
                there_x = (x + d % 4) % 4
                send(
                    s4.at[c, (there_z % 2) * 8 + there_c * 4 + there_x], r1.at[c, me],
                    s1_send.at[c], s1_recv.at[c], (there_z * 2 + there_c, y * 4 + there_x),
                )
                return carry

            mine = (z % 2) * 8 + core * 4 + x
        lax.fori_loop(1, 32, push, 0)
        for a in range(2):
            for b in range(2):
                r1[c, me, a, b] = s4[c, mine, a, b]

    def out_last(c):
        left, half = c // 2, c % 2
        wait_for(r1.at[c, pl.ds(0, 31)], s1_recv.at[c])
        got, pos = (gz, z) if half == 0 else (gy, y)
        for d in (2, 1, 3):
            there = (pos + d) % 4
            target = (there * 2 + core, big_y) if half == 0 else (big_x, there * 4 + x)
            send(r1.at[c, :, there % 2], got.at[left, pos], s2_send.at[c], s2_recv.at[c], target)
        own = pltpu.make_async_copy(r1.at[c, :, pos % 2], got.at[left, pos], own_sem.at[c])
        own.start()

    def finish(c):
        left, half = c // 2, c % 2
        got, pos = (gz, z) if half == 0 else (gy, y)
        wait_for(got.at[left, pl.ds(0, 3)], s2_recv.at[c])
        pltpu.make_async_copy(r1.at[c, :, pos % 2], got.at[left, pos], own_sem.at[c]).wait()

    pass_on(0)
    levels(0)
    out_first(0)
    pass_on(1)
    levels(1)
    out_first(1)
    pass_on(2)
    out_last(0)
    levels(2)
    out_first(2)
    pass_on(3)
    out_last(1)
    levels(3)
    out_first(3)
    out_last(2)
    out_last(3)
    for c in range(4):
        finish(c)
        wait_for(sendx.at[c, pl.ds(0, 3)], x_send.at[c])
        wait_for(send1.at[c, pl.ds(0, 31)], in_send.at[c])
        wait_for(r1.at[c, pl.ds(0, 31)], s1_send.at[c])
        wait_for(gz.at[0, pl.ds(0, 3)], s2_send.at[c])
    wait_for(p1.at[pl.ds(0, 31)], ph_send.at[0])
    wait_for(phs.at[:, pl.ds(0, 3)], ph_send.at[1])


def exchange(coeffs, phases, spread):
    half = jax.ShapeDtypeStruct((2, 4, 32, 2, 8, WIDE), F32)
    dma = pltpu.SemaphoreType.DMA
    return pl.pallas_call(
        exchange_kernel,
        out_shape=(half, half),
        in_specs=[
            pl.BlockSpec(memory_space=pl.ANY),
            pl.BlockSpec(memory_space=pl.ANY),
            pl.BlockSpec(memory_space=pltpu.VMEM),
        ],
        out_specs=(pl.BlockSpec(memory_space=pl.ANY), pl.BlockSpec(memory_space=pl.ANY)),
        scratch_shapes=[
            pltpu.VMEM((2, 128, 2, 16, WIDE), F32),
            pltpu.VMEM((128, 8, WIDE), F32),
            pltpu.VMEM((2, 128, 8, WIDE), F32),
            pltpu.VMEM((2, 128, 8, WIDE), F32),
            pltpu.VMEM((4, 4, 32, 8, WIDE), F32),
            pltpu.VMEM((4, 4, 32, 8, WIDE), F32),
            pltpu.VMEM((4, 32, 2, 8, WIDE), F32),
            pltpu.VMEM((4, 32, 2, 8, WIDE), F32),
            pltpu.VMEM((32, 4, 8, WIDE), F32),
            pltpu.VMEM((32, 4, 8, WIDE), F32),
            pltpu.VMEM((2, 128, 8, WIDE), F32),
            pltpu.VMEM((2, 128, 8, WIDE), F32),
            pltpu.VMEM((512, 3 * WIDE), BF16),
            pltpu.VMEM((512, 4 * WIDE), F32),
            pltpu.VMEM((4, 16, 2, 2, 8, WIDE), F32),
            pltpu.VMEM((4, 32, 2, 2, 8, WIDE), F32),
            dma((3,)),
            dma((4,)),
            dma((4,)),
            dma((4,)),
            dma((4,)),
            dma((4,)),
            dma((4,)),
            dma((4,)),
            dma((4,)),
            dma((4,)),
            dma((2,)),
            dma((2,)),
        ],
        compiler_params=pltpu.CompilerParams(
            collective_id=0, has_side_effects=True, vmem_limit_bytes=48 * 2**20
        ),
        name="exchange",
    )(coeffs, phases, spread)


def field_kernel(gz, gy, angles, w_ref, out, cos_f, sin_f):
    q = lax.axis_index("qx") // 4
    s = lax.axis_index("qy") // 8
    cos, sin = turn_tables(angles[0], False)
    for k in range(2):
        cos_f[k] = cos[k]
        sin_f[k] = sin[k]
    matrix = w_ref.at[q * 2 + s]

    def step(sy, carry):
        pieces = []
        for sx in range(4):
            for left in range(2):
                for k in range(2):
                    pieces.append(gz[left, 0, sy * 4 + sx, k])
                    pieces.append(gy[left, sy, sx, k])
        high, low = split_parts(jnp.concatenate(pieces, axis=0))
        both = jnp.dot(
            jnp.concatenate([high, low, high], axis=1), matrix[...], preferred_element_type=F32
        )
        at = 0
        for sx in range(4):
            for left in range(2):
                row = pl.ds((sy * 4 + sx) * 2 + left, 1)
                for k in range(2):
                    direct = both[at : at + 16, :WIDE]
                    crossed = both[at : at + 16, WIDE:]
                    out[0, sy * 4 + sx, left, k] = direct * cos_f[k, row, :] + crossed * sin_f[k, row, :]
                    at += 16
        return carry

    lax.fori_loop(0, 4, step, 0)


def evaluate_field(gz, gy, angles, last):
    return pl.pallas_call(
        field_kernel,
        grid=(8,),
        out_shape=jax.ShapeDtypeStruct((8, 16, 2, 2, 16, WIDE), F32),
        in_specs=[
            pl.BlockSpec((2, 1, 16, 2, 8, WIDE), lambda h: (0, h // 2, h % 2, 0, 0, 0)),
            pl.BlockSpec((2, 4, 4, 2, 8, WIDE), lambda h: (0, 0, h, 0, 0, 0)),
            pl.BlockSpec((1, 32, WIDE), lambda h: (h, 0, 0)),
            pl.BlockSpec((4, 3 * WIDE, 2 * WIDE), lambda h: (0, 0, 0)),
        ],
        out_specs=pl.BlockSpec((1, 16, 2, 2, 16, WIDE), lambda h: (h, 0, 0, 0, 0, 0)),
        scratch_shapes=[pltpu.VMEM((2, 32, WIDE), F32), pltpu.VMEM((2, 32, WIDE), F32)],
        compiler_params=pltpu.CompilerParams(vmem_limit_bytes=32 * 2**20),
        name="field",
    )(gz, gy, angles, last)


def per_device(coeffs, level_phase, field_phase):
    spread, last = weights()
    gz, gy = exchange(
        coeffs.reshape(128, 2, 2, 16, WIDE), level_phase.reshape(128, 8, WIDE), spread
    )
    field = evaluate_field(gz, gy, field_phase.reshape(8, 32, WIDE), last)
    return field.reshape(coeffs.shape)


def solution(mesh):
    return jax.shard_map(
        per_device,
        mesh=mesh,
        in_specs=(
            P("qx", "qy", None, None, None, None, None, None),
            P("qx", "qy", None, None, None, None, None),
            P("qx", "qy", None, None, None, None),
        ),
        out_specs=P("qx", "qy", None, None, None, None, None, None),
        check_vma=False,
    )
```

time: 584 us -> 148 us (0.25)
  waiting for transfers between devices: 494 us -> 0 us
  Pallas kernels: 0 us -> 146 us
  other arithmetic: 30.6 us -> 0 us
  matrix products: 28.4 us -> 0 us
  starting transfers between devices: 15.8 us -> 0 us
  local copies, waits for them, and re-layouts: 11.4 us -> 2.12 us
    ppermute x7 -> x0, waiting for transfers between devices: 494 us -> none  [from_partner(): return lax.ppermute(value, axis, pairs)]
    pallas_call x0 -> x2, Pallas kernels: none -> 146 us  [the longest x1 136 us: exchange(): pl.pallas_call(exchange_kernel, out_shape=(half, half), in_specs=[pl.Bloc...]
    dot_general x6 -> x0, matrix products: 28.4 us -> none  [the longest x3 17.9 us: pair_level(): return jnp.matmul(total, matrix, precision=lax.Precision.HIGHEST)]
    ppermute x7 -> x0, starting transfers between devices: 15.8 us -> none  [from_partner(): return lax.ppermute(value, axis, pairs)]
    sub x5 -> x0, other arithmetic: 12.1 us -> none  [rotate(): cosine * real_part - sine * imag_part]
    add x3 -> x0, other arithmetic: 10.6 us -> none  [pair_level(): partial_value = rotated + cross_x(rotated, x_bit)]
    cos x8 -> x0, local copies, waits for them, and re-layouts: 10 us -> none  [rotate(): cosine = jnp.cos(angles)]
    concatenate x4 -> x0, other arithmetic: 6.61 us -> none  [rotate(): jnp.concatenate([cosine * real_part - sine * imag_part, sine * real_part...]
  transfers between devices with their start and end apart: 7 -> 0, of which waited for: 7 -> 0; matrix products, arithmetic and copies ran while one was open for 0% -> 0% of each run, Pallas kernels for 0% -> 0%
where the time goes in v2:
time: 148 us
  Pallas kernels  146 us (99%)
  local copies, waits for them, and re-layouts  2.12 us (1%)
    pallas_call x1, Pallas kernels, exchange(): pl.pallas_call(exchange_kernel, out_shape=(half, half), in_specs=[pl.Bloc...  136 us
    pallas_call x1, Pallas kernels, evaluate_field(): pl.pallas_call(field_kernel, grid=(8,), out_shape=jax.ShapeDtypeStruct((8...  9.38 us

profile of v2, /device:TPU:1, one launch (start us, length us, event | category | flops | bytes accessed | tf_op | source)
XLA Modules:
  0.0 147.7 jit_solution(5241035004518515771)
XLA Ops:
  0.0 0.0 copy-start
  0.0 0.0 copy-start.1
  0.0 1.1 copy-done.1
  1.1 0.0 copy-start.2
  1.1 1.0 copy-done.2
  2.1 0.0 copy-start.3
  2.1 136.2 %exchange.1 = (f32[2,4,32,2,8,128]{5,4,3,2,1,0:T(8,128)S(1)}, f32[2,4,32,2,8,128]{5,4,3,2,1,0:T(8,128)S(1)}) custom-call(f32[128,2,2,16,128]{4,3,2,1,0:T(8,128)} %bitcast.6, f32[128,8,128]{2,1,0:T(8,128)S(1)} %bitcast.4, bf16[384,512]{1,0:T(8,128)(2,1)S(1)} %copy-done.2), custom_call_target="tpu_custom_call" | custom-call | tf_op jit(solution)/shard_map/exchange/pallas_call | solution.py:425
  138.3 0.0 copy-done
  138.3 0.0 copy-done.3
  138.3 9.4 %field.1 = f32[8,16,2,2,16,128]{5,4,3,2,1,0:T(8,128)} custom-call(f32[2,4,32,2,8,128]{5,4,3,2,1,0:T(8,128)S(1)} %get-tuple-element.7.gz, f32[2,4,32,2,8,128]{5,4,3,2,1,0:T(8,128)S(1)} %get-tuple-element.8.gy, f32[8,32,128]{2,1,0:T(8,128)S(1)} %bitcast.5, bf16[4,384,256]{2,1,0:T(8,128)(2,1)S(1)} %copy-done), custom_call_target="tpu_custom_call" | custom-call | tf_op jit(solution)/shard_map/field/pallas_call | solution.py:506
Async XLA Ops:
  0.0 138.3 %copy-start = (bf16[4,384,256]{2,1,0:T(8,128)(2,1)S(1)}, bf16[4,384,256]{2,1,0:T(8,128)(2,1)}, u32[]{:S(2)}) copy-start(bf16[4,384,256]{2,1,0:T(8,128)(2,1)} %constant.5.clone.w_ref) | copy-start | bytes 2359300
  0.0 1.1 copy-start.1
  1.1 1.0 copy-start.2
  2.1 136.2 %copy-start.3 = (f32[1,1,8,16,2,128]{5,4,3,2,1,0:T(2,128)S(1)}, f32[1,1,8,16,2,128]{5,4,3,2,1,0:T(2,128)}, u32[]{:S(2)}) copy-start(f32[1,1,8,16,2,128]{5,4,3,2,1,0:T(2,128)} %param.7) | copy-start | bytes 393220

commit v3 on v2

--- a/solution.py
+++ b/solution.py
@@ -14,6 +14,7 @@
 MESH = pl.DeviceIdType.MESH
 F32 = jnp.float32
 BF16 = jnp.bfloat16
+DIGITS = [(a, b, c) for a in range(2) for b in range(2) for c in range(2)]
 
 
 def point_tables(count):
@@ -114,8 +115,14 @@
         load.start()
         loads.append(load)
 
-    def device(dz, dc, dy, dx):
-        return ((z + dz) % 4) * 2 + (core + dc) % 2, ((y + dy) % 4) * 4 + (x + dx) % 4
+    zs = [(z + d) % 4 for d in range(4)]
+    cs = [core, 1 - core]
+    ys = [(y + d) % 4 for d in range(4)]
+    xs_ = [(x + d) % 4 for d in range(4)]
+    y_odd = [(y + d) % 2 for d in range(4)]
+    z_odd = [(z + d) % 2 for d in range(4)]
+    dev_x = [[zs[dz] * 2 + cs[dc] for dc in range(2)] for dz in range(4)]
+    dev_y = [[ys[dy] * 4 + xs_[dx] for dx in range(4)] for dy in range(4)]
 
     barrier = pltpu.get_barrier_semaphore()
     greeted = 0
@@ -125,7 +132,7 @@
                 for dx in range(4):
                     if (dz, dc, dy, dx) != (0, 0, 0, 0) and 0 in (dz, dy, dx):
                         pl.semaphore_signal(
-                            barrier, inc=1, device_id=device(dz, dc, dy, dx), device_id_type=MESH
+                            barrier, inc=1, device_id=(dev_x[dz][dc], dev_y[dy][dx]), device_id_type=MESH
                         )
                         greeted += 1
 
@@ -138,22 +145,25 @@
     phase_load.wait()
 
     def first_tables(i, carry):
-        cos, sin = turn_tables(lpv[i], True)
+        some = pl.ds(i * 8, 8)
+        cos, sin = turn_tables(lpv[some], True)
         for k in range(2):
-            cos1[k, i] = cos[k]
-            sin1[k, i] = sin[k]
+            cos1[k, some] = cos[k]
+            sin1[k, some] = sin[k]
         return carry
 
-    lax.fori_loop(0, 128, first_tables, 0)
+    lax.fori_loop(0, 16, first_tables, 0)
 
     def rotate_first(c):
         left, half = c // 2, c % 2
         if half == 0:
             loads[left].wait()
 
-        def step(i, carry):
-            for vx in range(4):
-                box = i * 4 + vx
+        def step(j, carry):
+            for n in range(16):
+                i = j * 4 + n // 4
+                vx = n % 4
+                box = j * 16 + n
                 direct = None
                 crossed = None
                 for k in range(2):
@@ -165,11 +175,11 @@
                 sendx[c, vx, i] = direct + swap(crossed)
             return carry
 
-        lax.fori_loop(0, 32, step, 0)
+        lax.fori_loop(0, 8, step, 0)
 
     def send_x(c):
         for dx in range(1, 4):
-            there = (x + dx) % 4
+            there = xs_[dx]
             send(sendx.at[c, there], recvx.at[c, x], x_send.at[c], x_recv.at[c], (big_x, y * 4 + there))
 
     rotate_first(0)
@@ -178,16 +188,12 @@
 
     me_in = big_x * 4 + y
 
-    def send_phase(d, carry):
-        there_x = ((z + d // 8) % 4) * 2 + (core + (d // 4) % 2) % 2
-        there_y = (y + d % 4) % 4
+    for d in range(1, 32):
+        there_x = dev_x[d // 8][(d // 4) % 2]
         send(
-            lpv.at[pl.ds((there_x * 4 + there_y) * 4, 4)], p1.at[me_in], ph_send.at[0], ph_recv.at[0],
-            (there_x, there_y * 4 + x),
+            lpv.at[pl.ds(there_x * 16 + ys[d % 4] * 4, 4)], p1.at[me_in], ph_send.at[0], ph_recv.at[0],
+            (there_x, dev_y[d % 4][0]),
         )
-        return carry
-
-    lax.fori_loop(1, 32, send_phase, 0)
     for vx in range(4):
         p1[me_in, vx] = lpv[me_in * 4 + vx]
 
@@ -196,36 +202,29 @@
         if c == 1:
             wait_for(p1.at[pl.ds(0, 31)], ph_recv.at[0])
             for dx in range(1, 4):
-                there = (x + dx) % 4
+                there = xs_[dx]
                 send(p1.at[:, there], phs.at[:, x], ph_send.at[1], ph_recv.at[1], (big_x, y * 4 + there))
         send_x(c)
 
     def pass_on(c):
         wait_for(recvx.at[c, pl.ds(0, 3)], x_recv.at[c])
 
-        def own(i, carry):
-            recvx[c, x, i] = sendx[c, x, i]
-            return carry
-
-        lax.fori_loop(0, 32, own, 0)
-
-        def add(i, carry):
+        recvx[c, x] = sendx[c, x]
+
+        def add(j, carry):
+            some = pl.ds(j * 8, 8)
             for y1 in range(2):
-                send1[c, i, y1] = recvx[c, 2 * y1, i] + recvx[c, 2 * y1 + 1, i]
-            return carry
-
-        lax.fori_loop(0, 32, add, 0)
-
-        def push(d, carry):
-            there_x = ((z + d // 8) % 4) * 2 + (core + (d // 4) % 2) % 2
-            there_y = (y + d % 4) % 4
+                send1[c, some, y1] = recvx[c, 2 * y1, some] + recvx[c, 2 * y1 + 1, some]
+            return carry
+
+        lax.fori_loop(0, 4, add, 0)
+
+        for d in range(1, 32):
+            there_x = dev_x[d // 8][(d // 4) % 2]
             send(
-                send1.at[c, there_x * 4 + there_y], recv1.at[c, me_in], in_send.at[c], in_recv.at[c],
-                (there_x, there_y * 4 + x),
+                send1.at[c, there_x * 4 + ys[d % 4]], recv1.at[c, me_in], in_send.at[c], in_recv.at[c],
+                (there_x, dev_y[d % 4][0]),
             )
-            return carry
-
-        lax.fori_loop(1, 32, push, 0)
         for y1 in range(2):
             recv1[c, me_in, y1] = send1[c, me_in, y1]
 
@@ -259,119 +258,105 @@
         left, half = c // 2, c % 2
         wait_for(recv1.at[c, pl.ds(0, 31)], in_recv.at[c])
 
-        def first(i, carry):
-            put_parts(i * 16, recv1[c, i].reshape(16, WIDE))
-            return carry
-
-        lax.fori_loop(0, 32, first, 0)
+        def first(j, carry):
+            for n in range(8):
+                i = j * 8 + n
+                put_parts(i * 16, recv1[c, i].reshape(16, WIDE))
+            return carry
+
+        lax.fori_loop(0, 4, first, 0)
         multiply()
         if c == 0:
             phase_tables()
 
-        def second(t, carry):
-            x2, x1, y3, y2 = t // 8, (t // 4) % 2, (t // 2) % 2, t % 2
-            for y0 in range(2):
+        def second(a, carry):
+            for y3, y2, y0 in DIGITS:
                 outs = []
                 for k in range(2):
                     parts = []
                     for x0 in range(2):
                         for y1 in range(2):
-                            block = x2 * 32 + x1 * 16 + x0 * 8 + y3 * 4 + y2 * 2 + y1
-                            place = (x2 * 4 + x1 * 2 + x0) * 16 + y3 * 8 + y2 * 4 + y1 * 2 + y0
+                            block = a * 16 + (x0 * 8 + y3 * 4 + y2 * 2 + y1)
+                            place = a * 32 + (x0 * 16 + y3 * 8 + y2 * 4 + y1 * 2 + y0)
                             parts.append((block, k * 2 + y0, k, place))
                     outs.append(turned_sum(parts, 2 + left))
-                put_parts((t * 2 + y0) * 16, jnp.concatenate(outs, axis=0))
-            return carry
-
-        lax.fori_loop(0, 16, second, 0)
+                put_parts(a * 128 + (y3 * 4 + y2 * 2 + y0) * 16, jnp.concatenate(outs, axis=0))
+            return carry
+
+        lax.fori_loop(0, 4, second, 0)
         multiply()
 
-        def third(t, carry):
-            x2, y3, y0, k = t // 8, (t // 4) % 2, (t // 2) % 2, t % 2
-            for x0 in range(2):
-                outs = []
-                for y1 in range(2):
-                    parts = []
-                    for x1 in range(2):
-                        for y2 in range(2):
-                            block = x2 * 32 + x1 * 16 + y3 * 8 + y2 * 4 + y0 * 2 + k
-                            place = (x2 * 4 + x1 * 2 + x0) * 16 + y3 * 8 + y2 * 4 + y1 * 2 + y0
-                            parts.append((block, x0 * 2 + y1, k, place))
-                    outs.append(turned_sum(parts, 4 + left))
-                put_parts((t * 2 + x0) * 16, jnp.concatenate(outs, axis=0))
-            return carry
-
-        lax.fori_loop(0, 16, third, 0)
+        def third(x2, carry):
+            for y3, y0, k in DIGITS:
+                for x0 in range(2):
+                    outs = []
+                    for y1 in range(2):
+                        parts = []
+                        for x1 in range(2):
+                            for y2 in range(2):
+                                block = x2 * 32 + (x1 * 16 + y3 * 8 + y2 * 4 + y0 * 2 + k)
+                                place = x2 * 64 + (x1 * 32 + x0 * 16 + y3 * 8 + y2 * 4 + y1 * 2 + y0)
+                                parts.append((block, x0 * 2 + y1, k, place))
+                        outs.append(turned_sum(parts, 4 + left))
+                    put_parts(
+                        x2 * 256 + (y3 * 8 + y0 * 4 + k * 2 + x0) * 16, jnp.concatenate(outs, axis=0)
+                    )
+            return carry
+
+        lax.fori_loop(0, 2, third, 0)
         multiply()
 
-        def fourth(t, carry):
-            y0, k, x0, y1 = t // 8, (t // 4) % 2, (t // 2) % 2, t % 2
-            for x1 in range(2):
-                for y2 in range(2):
-                    parts = []
-                    for x2 in range(2):
-                        for y3 in range(2):
-                            block = x2 * 32 + y3 * 16 + y0 * 8 + k * 4 + x0 * 2 + y1
-                            place = (x2 * 4 + x1 * 2 + x0) * 16 + y3 * 8 + y2 * 4 + y1 * 2 + y0
-                            parts.append((block, x1 * 2 + y2, k, place))
-                    if half == 0:
-                        s4[c, x0 * 8 + y2 * 4 + y1 * 2 + y0, x1, k] = turned_sum(parts, 6 + left)
-                    else:
-                        s4[c, x1 * 8 + x0 * 4 + y1 * 2 + y0, y2, k] = turned_sum(parts, 6 + left)
-            return carry
-
-        lax.fori_loop(0, 16, fourth, 0)
+        def fourth(y0, carry):
+            for k, x0, y1 in DIGITS:
+                for x1 in range(2):
+                    for y2 in range(2):
+                        parts = []
+                        for x2 in range(2):
+                            for y3 in range(2):
+                                block = y0 * 8 + (x2 * 32 + y3 * 16 + k * 4 + x0 * 2 + y1)
+                                place = y0 + (x2 * 64 + x1 * 32 + x0 * 16 + y3 * 8 + y2 * 4 + y1 * 2)
+                                parts.append((block, x1 * 2 + y2, k, place))
+                        if half == 0:
+                            s4[c, y0 + (x0 * 8 + y2 * 4 + y1 * 2), x1, k] = turned_sum(parts, 6 + left)
+                        else:
+                            s4[c, y0 + (x1 * 8 + x0 * 4 + y1 * 2), y2, k] = turned_sum(parts, 6 + left)
+            return carry
+
+        lax.fori_loop(0, 2, fourth, 0)
 
     def phase_tables():
         wait_for(phs.at[:, pl.ds(0, 3)], ph_recv.at[1])
 
-        def own(i, carry):
-            phs[i, x] = p1[i, x]
-            return carry
-
-        lax.fori_loop(0, 32, own, 0)
+        phs[:, x] = p1[:, x]
 
         def table(i, carry):
-            for sx in range(4):
-                cos, sin = turn_tables(phs[i, sx], True)
-                for k in range(2):
-                    cos_t[k, i * 4 + sx] = cos[k]
-                    sin_t[k, i * 4 + sx] = sin[k]
-            return carry
-
-        lax.fori_loop(0, 32, table, 0)
+            some = pl.ds(i * 8, 8)
+            angle = phs[pl.ds(i * 2, 2)].reshape(8, 8, WIDE)
+            cos, sin = turn_tables(angle, True)
+            for k in range(2):
+                cos_t[k, some] = cos[k]
+                sin_t[k, some] = sin[k]
+            return carry
+
+        lax.fori_loop(0, 16, table, 0)
 
     def out_first(c):
         half = c % 2
         if half == 0:
             me = core * 16 + y * 4 + x
-
-            def push(d, carry):
-                there_c = (core + d // 16) % 2
-                there_y = (y + (d // 4) % 4) % 4
-                there_x = (x + d % 4) % 4
-                send(
-                    s4.at[c, there_c * 8 + (there_y % 2) * 4 + there_x], r1.at[c, me],
-                    s1_send.at[c], s1_recv.at[c], (z * 2 + there_c, there_y * 4 + there_x),
-                )
-                return carry
-
             mine = core * 8 + (y % 2) * 4 + x
         else:
             me = (z * 2 + core) * 4 + x
-
-            def push(d, carry):
-                there_c = (core + d // 16) % 2
-                there_z = (z + (d // 4) % 4) % 4
-                there_x = (x + d % 4) % 4
-                send(
-                    s4.at[c, (there_z % 2) * 8 + there_c * 4 + there_x], r1.at[c, me],
-                    s1_send.at[c], s1_recv.at[c], (there_z * 2 + there_c, y * 4 + there_x),
-                )
-                return carry
-
             mine = (z % 2) * 8 + core * 4 + x
-        lax.fori_loop(1, 32, push, 0)
+        for d in range(1, 32):
+            dc, dx, dt = d // 16, d % 4, (d // 4) % 4
+            if half == 0:
+                there = cs[dc] * 8 + y_odd[dt] * 4 + xs_[dx]
+                target = (dev_x[0][dc], dev_y[dt][dx])
+            else:
+                there = z_odd[dt] * 8 + cs[dc] * 4 + xs_[dx]
+                target = (dev_x[dt][dc], dev_y[0][dx])
+            send(s4.at[c, there], r1.at[c, me], s1_send.at[c], s1_recv.at[c], target)
         for a in range(2):
             for b in range(2):
                 r1[c, me, a, b] = s4[c, mine, a, b]
@@ -381,9 +366,9 @@
         wait_for(r1.at[c, pl.ds(0, 31)], s1_recv.at[c])
         got, pos = (gz, z) if half == 0 else (gy, y)
         for d in (2, 1, 3):
-            there = (pos + d) % 4
-            target = (there * 2 + core, big_y) if half == 0 else (big_x, there * 4 + x)
-            send(r1.at[c, :, there % 2], got.at[left, pos], s2_send.at[c], s2_recv.at[c], target)
+            odd = z_odd[d] if half == 0 else y_odd[d]
+            target = (dev_x[d][0], big_y) if half == 0 else (big_x, dev_y[d][0])
+            send(r1.at[c, :, odd], got.at[left, pos], s2_send.at[c], s2_recv.at[c], target)
         own = pltpu.make_async_copy(r1.at[c, :, pos % 2], got.at[left, pos], own_sem.at[c])
         own.start()
 

time: 148 us -> 111 us (0.75)
  Pallas kernels: 146 us -> 107 us
    pallas_call x1, Pallas kernels: 136 us -> 97.9 us  [exchange(): pl.pallas_call(exchange_kernel, out_shape=(half, half), in_specs=[pl.Bloc...]
where the time goes in v3:
time: 111 us; the launch traced here: 109 us
  Pallas kernels  107 us (96%)
  local copies, waits for them, and re-layouts  2.12 us (2%)
    pallas_call x1, Pallas kernels, exchange(): pl.pallas_call(exchange_kernel, out_shape=(half, half), in_specs=[pl.Bloc...  97.9 us
    pallas_call x1, Pallas kernels, evaluate_field(): pl.pallas_call(field_kernel, grid=(8,), out_shape=jax.ShapeDtypeStruct((8...  9.38 us

profile of v3, /device:TPU:1, one launch (start us, length us, event | category | flops | bytes accessed | tf_op | source)
XLA Modules:
  0.0 109.5 jit_solution(1139129990780558287)
XLA Ops:
  0.0 0.0 copy-start
  0.0 0.0 copy-start.1
  0.0 1.1 %copy-done.1 = f32[1,1,8,16,4,2,128]{6,5,4,3,2,1,0:T(2,128)S(1)} copy-done((f32[1,1,8,16,4,2,128]{6,5,4,3,2,1,0:T(2,128)S(1)}, f32[1,1,8,16,4,2,128]{6,5,4,3,2,1,0:T(2,128)}, u32[]{:S(2)}) %copy-start.1) | copy-done | bytes 524312
  1.1 0.0 copy-start.2
  1.1 1.0 copy-done.2
  2.1 0.0 copy-start.3
  2.1 97.9 %exchange.1 = (f32[2,4,32,2,8,128]{5,4,3,2,1,0:T(8,128)S(1)}, f32[2,4,32,2,8,128]{5,4,3,2,1,0:T(8,128)S(1)}) custom-call(f32[128,2,2,16,128]{4,3,2,1,0:T(8,128)} %bitcast.6, f32[128,8,128]{2,1,0:T(8,128)S(1)} %bitcast.4, bf16[384,512]{1,0:T(8,128)(2,1)S(1)} %copy-done.2), custom_call_target="tpu_custom_call" | custom-call | tf_op jit(solution)/shard_map/exchange/pallas_call | solution.py:410
  100.1 0.0 copy-done
  100.1 0.0 copy-done.3
  100.1 9.4 %field.1 = f32[8,16,2,2,16,128]{5,4,3,2,1,0:T(8,128)} custom-call(f32[2,4,32,2,8,128]{5,4,3,2,1,0:T(8,128)S(1)} %get-tuple-element.7.gz, f32[2,4,32,2,8,128]{5,4,3,2,1,0:T(8,128)S(1)} %get-tuple-element.8.gy, f32[8,32,128]{2,1,0:T(8,128)S(1)} %bitcast.5, bf16[4,384,256]{2,1,0:T(8,128)(2,1)S(1)} %copy-done), custom_call_target="tpu_custom_call" | custom-call | tf_op jit(solution)/shard_map/field/pallas_call | solution.py:491
Async XLA Ops:
  0.0 100.1 %copy-start = (bf16[4,384,256]{2,1,0:T(8,128)(2,1)S(1)}, bf16[4,384,256]{2,1,0:T(8,128)(2,1)}, u32[]{:S(2)}) copy-start(bf16[4,384,256]{2,1,0:T(8,128)(2,1)} %constant.5.clone.w_ref) | copy-start | bytes 2359300
  0.0 1.1 %copy-start.1 = (f32[1,1,8,16,4,2,128]{6,5,4,3,2,1,0:T(2,128)S(1)}, f32[1,1,8,16,4,2,128]{6,5,4,3,2,1,0:T(2,128)}, u32[]{:S(2)}) copy-start(f32[1,1,8,16,4,2,128]{6,5,4,3,2,1,0:T(2,128)} %param.6) | copy-start | bytes 1572868
  1.1 1.0 copy-start.2
  2.1 98.0 %copy-start.3 = (f32[1,1,8,16,2,128]{5,4,3,2,1,0:T(2,128)S(1)}, f32[1,1,8,16,2,128]{5,4,3,2,1,0:T(2,128)}, u32[]{:S(2)}) copy-start(f32[1,1,8,16,2,128]{5,4,3,2,1,0:T(2,128)} %param.7) | copy-start | bytes 393220

commit v4 on v3

v4 whole, which is shorter than its diff:
```python
import functools

import jax
import jax.numpy as jnp
import numpy as np
from jax import lax
from jax.experimental import pallas as pl
from jax.experimental.pallas import tpu as pltpu
from jax.sharding import PartitionSpec as P

CHEB = 8
PTS = CHEB * CHEB
WIDE = 2 * PTS
MESH = pl.DeviceIdType.MESH
F32 = jnp.float32
BF16 = jnp.bfloat16
DIGITS = [(a, b, c) for a in range(2) for b in range(2) for c in range(2)]


def point_tables(count):
    points = 0.5 - 0.5 * np.cos((2 * np.arange(count) + 1) * np.pi / (2 * count))

    def lagrange(places):
        values = np.ones((len(places), count))
        for k in range(count):
            for m in range(count):
                if m != k:
                    values[:, k] = values[:, k] * (places - points[m]) / (points[k] - points[m])
        return values

    halves = [lagrange((q + points) / 2.0) for q in range(2)]
    uniform = lagrange((np.arange(count) + 0.5) / count)
    identity = np.eye(2)
    children = [
        [np.kron(identity, np.kron(halves[q], halves[s])).T for s in range(2)] for q in range(2)
    ]
    evaluate = np.kron(identity, np.kron(uniform, uniform)).T
    return children, evaluate


def three_parts(matrix):
    high = matrix.astype(np.float32).astype(BF16)
    low = (matrix - high.astype(np.float64)).astype(np.float32).astype(BF16)
    return np.concatenate([high, high, low], axis=0)


def weights():
    children, evaluate = point_tables(CHEB)
    spread = three_parts(np.concatenate([children[q][s] for q in range(2) for s in range(2)], axis=1))
    last = []
    for q in range(2):
        for s in range(2):
            both = children[q][s] @ evaluate
            swapped = np.concatenate([both[:, PTS:], both[:, :PTS]], axis=1)
            last.append(three_parts(np.concatenate([both, swapped], axis=1)))
    return jnp.asarray(spread), jnp.asarray(np.stack(last))


def split_parts(value):
    high = value.astype(BF16)
    low = (value - high.astype(F32)).astype(BF16)
    return high, low


def sine_cosine(angle):
    u = angle * 0.5
    w = u * u
    s = -2.5052108e-08
    for c in (2.7557319e-06, -1.9841270e-04, 8.3333333e-03, -1.6666667e-01, 1.0):
        s = s * w + c
    s = s * u
    c_ = 2.0876757e-09
    for c in (-2.7557319e-07, 2.4801587e-05, -1.3888889e-03, 4.1666667e-02, -0.5, 1.0):
        c_ = c_ * w + c
    return 2.0 * s * c_, 1.0 - 2.0 * s * s


def swap(value):
    return pltpu.roll(value, PTS, value.ndim - 1)


def turn_tables(angle, before):
    sine, cosine = sine_cosine(angle)
    lane = lax.broadcasted_iota(jnp.int32, angle.shape, angle.ndim - 1)
    low = lane < PTS
    cos_swap, sin_swap = swap(cosine), swap(sine)
    cos = (jnp.where(low, cosine, cos_swap), jnp.where(low, cos_swap, cosine))
    if before:
        sin = (jnp.where(low, sine, -sin_swap), jnp.where(low, sin_swap, -sine))
    else:
        sin = (jnp.where(low, -sine, sin_swap), jnp.where(low, -sin_swap, sine))
    return cos, sin


def wait_for(ref, sem):
    pltpu.make_async_copy(ref, ref, sem).wait()


def butterfly_kernel(
    coeffs, phases, field_phases, w_all, w_last, out,
    cbuf, lpv, fpv, w_ref, wf_ref, cos1, sin1, cos_f, sin_f,
    send_a, recv_xa, send_ya, recv_ya, send_yb, recv_yb, recv_xb,
    p1, phs, cos_t, sin_t, xs, res, s4, r1, gz, gy,
    load_sem, x_send, x_recv, in_send, in_recv, s1_send, s1_recv, s2_send, s2_recv, ph_send, ph_recv,
):
    big_x = lax.axis_index("qx")
    big_y = lax.axis_index("qy")
    z, core = big_x // 2, big_x % 2
    y, x = big_y // 4, big_y % 4
    pick = (z // 2) * 2 + y // 2

    loads = [
        pltpu.make_async_copy(src, dst, load_sem.at[n])
        for n, (src, dst) in enumerate(
            [
                (phases, lpv),
                (coeffs.at[:, 0], cbuf.at[0]),
                (coeffs.at[:, 1], cbuf.at[1]),
                (w_all, w_ref),
                (field_phases, fpv),
                (w_last.at[pick], wf_ref),
            ]
        )
    ]
    for load in loads:
        load.start()

    zs = [(z + d) % 4 for d in range(4)]
    cs = [core, 1 - core]
    ys = [(y + d) % 4 for d in range(4)]
    xs_ = [(x + d) % 4 for d in range(4)]
    y_odd = [(y + d) % 2 for d in range(4)]
    z_odd = [(z + d) % 2 for d in range(4)]
    dev_x = [[zs[dz] * 2 + cs[dc] for dc in range(2)] for dz in range(4)]
    dev_y = [[ys[dy] * 4 + xs_[dx] for dx in range(4)] for dy in range(4)]

    barrier = pltpu.get_barrier_semaphore()
    greeted = 0
    for dz in range(4):
        for dc in range(2):
            for dy in range(4):
                for dx in range(4):
                    if (dz, dc, dy, dx) != (0, 0, 0, 0) and 0 in (dz, dy, dx):
                        pl.semaphore_signal(
                            barrier, inc=1, device_id=(dev_x[dz][dc], dev_y[dy][dx]), device_id_type=MESH
                        )
                        greeted += 1

    def send(src, dst, send_sem, recv_sem, target):
        pltpu.make_async_remote_copy(
            src_ref=src, dst_ref=dst, send_sem=send_sem, recv_sem=recv_sem,
            device_id=target, device_id_type=MESH,
        ).start()

    me_in = big_x * 4 + y
    me_z = core * 16 + y * 4 + x
    me_y = big_x * 4 + x

    loads[0].wait()

    def first_tables(i, carry):
        some = pl.ds(i * 8, 8)
        cos, sin = turn_tables(lpv[some], True)
        for k in range(2):
            cos1[k, some] = cos[k]
            sin1[k, some] = sin[k]
        return carry

    lax.fori_loop(0, 16, first_tables, 0)

    def rotate_first(c):
        left, half = c // 2, c % 2
        if half == 0:
            loads[1 + left].wait()

        def step(j, carry):
            for n in range(16):
                i = j * 4 + n // 4
                vx = n % 4
                box = j * 16 + n
                direct = None
                crossed = None
                for k in range(2):
                    value = cbuf[left, box, k, pl.ds(half * 8, 8), :]
                    d = value * cos1[k, box, pl.ds(left, 1), :]
                    e = value * sin1[k, box, pl.ds(left, 1), :]
                    direct = d if direct is None else direct + d
                    crossed = e if crossed is None else crossed + e
                if left == 0:
                    send_a[half, vx, i] = direct + swap(crossed)
                else:
                    send_yb[half, i, vx] = direct + swap(crossed)
            return carry

        lax.fori_loop(0, 8, step, 0)

    def send_x(src, dst, send_sem, recv_sem):
        for dx in range(1, 4):
            send(src(xs_[dx]), dst, send_sem, recv_sem, (big_x, dev_y[0][dx]))

    def send_in(src, dst, send_sem, recv_sem):
        for d in range(1, 32):
            there_x = dev_x[d // 8][(d // 4) % 2]
            send(src(there_x * 4 + ys[d % 4]), dst, send_sem, recv_sem, (there_x, dev_y[d % 4][0]))

    def enter(c):
        h = c % 2
        if c < 2:
            send_x(lambda t: send_a.at[h, t], recv_xa.at[h, x], x_send.at[c], x_recv.at[c])
        else:
            send_in(lambda t: send_yb.at[h, t], recv_yb.at[h, me_in], in_send.at[c], in_recv.at[c])

    def pass_on(c):
        h = c % 2
        if c < 2:
            wait_for(recv_xa.at[h, pl.ds(0, 3)], x_recv.at[c])
            recv_xa[h, x] = send_a[h, x]

            def add(j, carry):
                some = pl.ds(j * 8, 8)
                for y1 in range(2):
                    send_ya[h, some, y1] = recv_xa[h, 2 * y1, some] + recv_xa[h, 2 * y1 + 1, some]
                return carry

            lax.fori_loop(0, 4, add, 0)
            send_in(lambda t: send_ya.at[h, t], recv_ya.at[h, me_in], in_send.at[c], in_recv.at[c])
            recv_ya[h, me_in] = send_ya[h, me_in]
        else:
            wait_for(recv_yb.at[h, pl.ds(0, 31)], in_recv.at[c])
            recv_yb[h, me_in] = send_yb[h, me_in]
            send_x(lambda t: recv_yb.at[h, :, t], recv_xb.at[h, x], x_send.at[c], x_recv.at[c])
            recv_xb[h, x] = recv_yb[h, :, x]

    def send_phases():
        send_in(lambda t: lpv.at[pl.ds(t * 4, 4)], p1.at[me_in], ph_send.at[0], ph_recv.at[0])
        p1[me_in] = lpv[pl.ds(me_in * 4, 4)]

    def pass_phases():
        wait_for(p1.at[pl.ds(0, 31)], ph_recv.at[0])
        send_x(lambda t: p1.at[:, t], phs.at[:, x], ph_send.at[1], ph_recv.at[1])
        phs[:, x] = p1[:, x]

    def phase_tables():
        wait_for(phs.at[:, pl.ds(0, 3)], ph_recv.at[1])

        def table(i, carry):
            some = pl.ds(i * 8, 8)
            angle = phs[pl.ds(i * 2, 2)].reshape(8, 8, WIDE)
            cos, sin = turn_tables(angle, True)
            for k in range(2):
                cos_t[k, some] = cos[k]
                sin_t[k, some] = sin[k]
            return carry

        lax.fori_loop(0, 16, table, 0)

    def field_tables():
        loads[4].wait()

        def table(i, carry):
            cos, sin = turn_tables(fpv[i], False)
            for k in range(2):
                cos_f[k, i] = cos[k]
                sin_f[k, i] = sin[k]
            return carry

        lax.fori_loop(0, 8, table, 0)

    def put_parts(row, value):
        high, low = split_parts(value)
        rows = pl.ds(pl.multiple_of(row, 16), 16)
        xs[rows, 0:WIDE] = high
        xs[rows, WIDE : 2 * WIDE] = low
        xs[rows, 2 * WIDE : 3 * WIDE] = high

    def multiply():
        def piece(i, carry):
            rows = pl.ds(pl.multiple_of(i * 256, 256), 256)
            res[rows, :] = jnp.dot(xs[rows, :], w_ref[...], preferred_element_type=F32)
            return carry

        lax.fori_loop(0, 2, piece, 0)

    def turned_sum(parts, row):
        direct = None
        crossed = None
        for block, column, k, place in parts:
            value = res[pl.ds(pl.multiple_of(block * 8, 8), 8), column * WIDE : (column + 1) * WIDE]
            d = value * cos_t[k, place, pl.ds(row, 1), :]
            e = value * sin_t[k, place, pl.ds(row, 1), :]
            direct = d if direct is None else direct + d
            crossed = e if crossed is None else crossed + e
        return direct + swap(crossed)

    def level_one(c):
        h = c % 2
        if c < 2:
            wait_for(recv_ya.at[h, pl.ds(0, 31)], in_recv.at[c])
        else:
            wait_for(recv_xb.at[h, pl.ds(0, 3)], x_recv.at[c])

        def first(j, carry):
            for n in range(8):
                i = j * 8 + n
                if c < 2:
                    value = recv_ya[h, i].reshape(16, WIDE)
                else:
                    value = jnp.concatenate(
                        [recv_xb[h, 2 * y1, i] + recv_xb[h, 2 * y1 + 1, i] for y1 in range(2)], axis=0
                    )
                put_parts(i * 16, value)
            return carry

        lax.fori_loop(0, 4, first, 0)
        multiply()

    def other_levels(c):
        left = c // 2

        def second(a, carry):
            for y3, y2, y0 in DIGITS:
                outs = []
                for k in range(2):
                    parts = []
                    for x0 in range(2):
                        for y1 in range(2):
                            block = a * 16 + (x0 * 8 + y3 * 4 + y2 * 2 + y1)
                            place = a * 32 + (x0 * 16 + y3 * 8 + y2 * 4 + y1 * 2 + y0)
                            parts.append((block, k * 2 + y0, k, place))
                    outs.append(turned_sum(parts, 2 + left))
                put_parts(a * 128 + (y3 * 4 + y2 * 2 + y0) * 16, jnp.concatenate(outs, axis=0))
            return carry

        lax.fori_loop(0, 4, second, 0)
        multiply()

        def third(x2, carry):
            for y3, y0, k in DIGITS:
                for x0 in range(2):
                    outs = []
                    for y1 in range(2):
                        parts = []
                        for x1 in range(2):
                            for y2 in range(2):
                                block = x2 * 32 + (x1 * 16 + y3 * 8 + y2 * 4 + y0 * 2 + k)
                                place = x2 * 64 + (x1 * 32 + x0 * 16 + y3 * 8 + y2 * 4 + y1 * 2 + y0)
                                parts.append((block, x0 * 2 + y1, k, place))
                        outs.append(turned_sum(parts, 4 + left))
                    put_parts(
                        x2 * 256 + (y3 * 8 + y0 * 4 + k * 2 + x0) * 16, jnp.concatenate(outs, axis=0)
                    )
            return carry

        lax.fori_loop(0, 2, third, 0)
        multiply()

        def fourth(y0, carry):
            for k, x0, y1 in DIGITS:
                for x1 in range(2):
                    for y2 in range(2):
                        parts = []
                        for x2 in range(2):
                            for y3 in range(2):
                                block = y0 * 8 + (x2 * 32 + y3 * 16 + k * 4 + x0 * 2 + y1)
                                place = y0 + (x2 * 64 + x1 * 32 + x0 * 16 + y3 * 8 + y2 * 4 + y1 * 2)
                                parts.append((block, x1 * 2 + y2, k, place))
                        if k == 0:
                            s4[c, 0, y0 + (x0 * 8 + y2 * 4 + y1 * 2), x1] = turned_sum(parts, 6 + left)
                        else:
                            s4[c, 1, y0 + (x1 * 8 + x0 * 4 + y1 * 2), y2] = turned_sum(parts, 6 + left)
            return carry

        lax.fori_loop(0, 2, fourth, 0)

        for d in range(1, 32):
            dc, dt, dx = d // 16, (d // 4) % 4, d % 4
            send(
                s4.at[c, 0, cs[dc] * 8 + y_odd[dt] * 4 + xs_[dx]], r1.at[c, 0, me_z],
                s1_send.at[c, 0], s1_recv.at[c, 0], (dev_x[0][dc], dev_y[dt][dx]),
            )
            send(
                s4.at[c, 1, z_odd[dt] * 8 + cs[dc] * 4 + xs_[dx]], r1.at[c, 1, me_y],
                s1_send.at[c, 1], s1_recv.at[c, 1], (dev_x[dt][dc], dev_y[0][dx]),
            )
        r1[c, 0, me_z] = s4[c, 0, core * 8 + y_odd[0] * 4 + x]
        r1[c, 1, me_y] = s4[c, 1, z_odd[0] * 8 + core * 4 + x]

    def out_last(c, k):
        wait_for(r1.at[c, k, pl.ds(0, 31)], s1_recv.at[c, k])
        for d in (2, 1, 3):
            if k == 0:
                send(
                    r1.at[c, 0, :, z_odd[d]], gz.at[c, z], s2_send.at[c, 0], s2_recv.at[c, 0],
                    (dev_x[d][0], big_y),
                )
            else:
                send(
                    r1.at[c, 1, :, y_odd[d]], gy.at[c, y], s2_send.at[c, 1], s2_recv.at[c, 1],
                    (big_x, dev_y[d][0]),
                )
        if k == 0:
            gz[c, z] = r1[c, 0, :, z_odd[0]]
        else:
            gy[c, y] = r1[c, 1, :, y_odd[0]]

    def finish(c, k):
        left, half = c // 2, c % 2
        got = gz if k == 0 else gy
        wait_for(got.at[c, pl.ds(0, 3)], s2_recv.at[c, k])

        def piece(p, carry):
            for a in range(2):
                for n in range(16):
                    put_parts((a * 16 + n) * 16, got[c, p * 2 + a, pl.ds(2 * n, 2)].reshape(16, WIDE))
            res[:, 0 : 2 * WIDE] = jnp.dot(xs[...], wf_ref[...], preferred_element_type=F32)
            for a in range(2):
                for n in range(32):
                    if k == 0:
                        box_h, box_v = p * 4 + (a * 2 + n // 16), n % 16
                    else:
                        box_h, box_v = n // 4, p * 8 + (a * 4 + n % 4)
                    rows = slice((a * 32 + n) * 8, (a * 32 + n + 1) * 8)
                    at = pl.ds(box_v * 2 + left, 1)
                    out[box_h * 16 + box_v, left, k, pl.ds(half * 8, 8), :] = (
                        res[rows, 0:WIDE] * cos_f[k, box_h, at, :]
                        + res[rows, WIDE : 2 * WIDE] * sin_f[k, box_h, at, :]
                    )
            return carry

        lax.fori_loop(0, 2, piece, 0)

    rotate_first(0)
    pl.semaphore_wait(barrier, greeted)
    enter(0)
    send_phases()
    rotate_first(1)
    enter(1)
    rotate_first(2)
    enter(2)
    pass_on(0)
    pass_phases()
    rotate_first(3)
    enter(3)
    pass_on(1)
    pass_on(2)
    loads[3].wait()
    field_tables()
    level_one(0)
    phase_tables()
    other_levels(0)
    level_one(1)
    pass_on(3)
    other_levels(1)
    out_last(0, 0)
    out_last(0, 1)
    level_one(2)
    other_levels(2)
    level_one(3)
    out_last(1, 0)
    out_last(1, 1)
    other_levels(3)
    out_last(2, 0)
    out_last(2, 1)
    loads[5].wait()
    finish(0, 0)
    finish(0, 1)
    out_last(3, 0)
    out_last(3, 1)
    for c in range(1, 4):
        finish(c, 0)
        finish(c, 1)
    for c in range(4):
        h = c % 2
        wait_for(recv_xa.at[h, pl.ds(0, 3)], x_send.at[c])
        wait_for((recv_ya if c < 2 else recv_yb).at[h, pl.ds(0, 31)], in_send.at[c])
        for k in range(2):
            wait_for(r1.at[c, k, pl.ds(0, 31)], s1_send.at[c, k])
            wait_for(gz.at[c, pl.ds(0, 3)], s2_send.at[c, k])
    wait_for(p1.at[pl.ds(0, 31)], ph_send.at[0])
    wait_for(phs.at[:, pl.ds(0, 3)], ph_send.at[1])


def butterfly(coeffs, phases, field_phases, spread, last):
    dma = pltpu.SemaphoreType.DMA
    tile = (8, WIDE)

    def vmem(*shape):
        return pltpu.VMEM(shape + tile, F32)

    return pl.pallas_call(
        butterfly_kernel,
        out_shape=jax.ShapeDtypeStruct((128, 2, 2, 16, WIDE), F32),
        in_specs=[pl.BlockSpec(memory_space=pltpu.HBM)] * 5,
        out_specs=pl.BlockSpec(memory_space=pltpu.VMEM),
        scratch_shapes=[
            pltpu.VMEM((2, 128, 2, 16, WIDE), F32),
            vmem(128),
            pltpu.VMEM((8, 32, WIDE), F32),
            pltpu.VMEM((3 * WIDE, 4 * WIDE), BF16),
            pltpu.VMEM((3 * WIDE, 2 * WIDE), BF16),
            vmem(2, 128),
            vmem(2, 128),
            pltpu.VMEM((2, 8, 32, WIDE), F32),
            pltpu.VMEM((2, 8, 32, WIDE), F32),
            vmem(2, 4, 32),
            vmem(2, 4, 32),
            vmem(2, 32, 2),
            vmem(2, 32, 2),
            vmem(2, 32, 4),
            vmem(2, 32, 4),
            vmem(2, 4, 32),
            vmem(32, 4),
            vmem(32, 4),
            vmem(2, 128),
            vmem(2, 128),
            pltpu.VMEM((512, 3 * WIDE), BF16),
            pltpu.VMEM((512, 4 * WIDE), F32),
            vmem(4, 2, 16, 2),
            vmem(4, 2, 32, 2),
            vmem(4, 4, 32),
            vmem(4, 4, 32),
            dma((6,)),
            dma((4,)),
            dma((4,)),
            dma((4,)),
            dma((4,)),
            dma((4, 2)),
            dma((4, 2)),
            dma((4, 2)),
            dma((4, 2)),
            dma((2,)),
            dma((2,)),
        ],
        compiler_params=pltpu.CompilerParams(
            collective_id=0, has_side_effects=True, vmem_limit_bytes=48 * 2**20
        ),
        name="butterfly",
    )(coeffs, phases, field_phases, spread, last)


def per_device(coeffs, level_phase, field_phase):
    spread, last = weights()
    field = butterfly(
        coeffs.reshape(128, 2, 2, 16, WIDE), level_phase.reshape(128, 8, WIDE),
        field_phase.reshape(8, 32, WIDE), spread, last,
    )
    return field.reshape(coeffs.shape)


def solution(mesh):
    return jax.shard_map(
        per_device,
        mesh=mesh,
        in_specs=(
            P("qx", "qy", None, None, None, None, None, None),
            P("qx", "qy", None, None, None, None, None),
            P("qx", "qy", None, None, None, None),
        ),
        out_specs=P("qx", "qy", None, None, None, None, None, None),
        check_vma=False,
    )
```

time: 111 us -> 84.2 us (0.76); the launches traced: 109 us -> 83.9 us
  Pallas kernels: 107 us -> 77.8 us
  local copies, waits for them, and re-layouts: 2.12 us -> 6.09 us
    pallas_call x2 -> x1, Pallas kernels: 107 us -> 77.8 us  [butterfly(): pl.pallas_call(butterfly_kernel, out_shape=jax.ShapeDtypeStruct((128, 2,...]
    unnamed x8 -> x9, local copies, waits for them, and re-layouts: 2.12 us -> 6.09 us
where the time goes in v4:
time: 84.2 us; the launch traced here: 83.9 us
  Pallas kernels  77.8 us (92%)
  local copies, waits for them, and re-layouts  6.09 us (7%)
    pallas_call x1, Pallas kernels, butterfly(): pl.pallas_call(butterfly_kernel, out_shape=jax.ShapeDtypeStruct((128, 2,...  77.8 us
    unnamed x9, local copies, waits for them, and re-layouts  6.09 us

profile of v4, /device:TPU:1, one launch (start us, length us, event | category | flops | bytes accessed | tf_op | source)
XLA Modules:
  0.0 83.9 jit_solution(2267405837091361905)
XLA Ops:
  0.0 0.0 copy-start
  0.0 1.1 %copy-done = bf16[4,384,256]{2,1,0:T(8,128)(2,1)S(1)} copy-done((bf16[4,384,256]{2,1,0:T(8,128)(2,1)S(1)}, bf16[4,384,256]{2,1,0:T(8,128)(2,1)}, u32[]{:S(2)}) %copy-start) | copy-done | bytes 786456
  1.1 0.0 copy-start.1
  1.1 1.0 %copy-done.1 = f32[1,1,8,16,4,2,128]{6,5,4,3,2,1,0:T(2,128)S(1)} copy-done((f32[1,1,8,16,4,2,128]{6,5,4,3,2,1,0:T(2,128)S(1)}, f32[1,1,8,16,4,2,128]{6,5,4,3,2,1,0:T(2,128)}, u32[]{:S(2)}) %copy-start.1) | copy-done | bytes 524312
  2.2 0.0 copy-start.2
  2.2 1.0 %copy-done.2 = bf16[384,512]{1,0:T(8,128)(2,1)S(1)} copy-done((bf16[384,512]{1,0:T(8,128)(2,1)S(1)}, bf16[384,512]{1,0:T(8,128)(2,1)}, u32[]{:S(2)}) %copy-start.2) | copy-done | bytes 393240
  3.2 0.0 copy-start.3
  3.2 0.9 %copy-done.3 = f32[1,1,8,16,2,128]{5,4,3,2,1,0:T(2,128)S(1)} copy-done((f32[1,1,8,16,2,128]{5,4,3,2,1,0:T(2,128)S(1)}, f32[1,1,8,16,2,128]{5,4,3,2,1,0:T(2,128)}, u32[]{:S(2)}) %copy-start.3) | copy-done | bytes 131096
  4.1 77.8 %butterfly.1 = f32[128,2,2,16,128]{4,3,2,1,0:T(8,128)S(1)} custom-call(f32[128,2,2,16,128]{4,3,2,1,0:T(8,128)} %bitcast.7, f32[128,8,128]{2,1,0:T(8,128)S(1)} %bitcast.5, f32[8,32,128]{2,1,0:T(8,128)S(1)} %bitcast.6, bf16[384,512]{1,0:T(8,128)(2,1)S(1)} %copy-done.2, bf16[4,384,256]{2,1,0:T(8,128)(2,1)S(1)} %copy-done), custom_call_target="tpu_custom_call" | custom-call | tf_op jit(solution)/shard_map/butterfly/pallas_call | solution.py:490
  81.9 2.0 %copy.7 = f32[1,1,8,16,2,2,16,128]{7,6,5,4,3,2,1,0:T(8,128)} copy(f32[1,1,8,16,2,2,16,128]{7,6,5,4,3,2,1,0:T(8,128)S(1)} %bitcast.4) | data formatting | bytes 8388608
Async XLA Ops:
  0.0 1.1 %copy-start = (bf16[4,384,256]{2,1,0:T(8,128)(2,1)S(1)}, bf16[4,384,256]{2,1,0:T(8,128)(2,1)}, u32[]{:S(2)}) copy-start(bf16[4,384,256]{2,1,0:T(8,128)(2,1)} %constant.5.clone.w_last) | copy-start | bytes 2359300
  1.1 1.0 %copy-start.1 = (f32[1,1,8,16,4,2,128]{6,5,4,3,2,1,0:T(2,128)S(1)}, f32[1,1,8,16,4,2,128]{6,5,4,3,2,1,0:T(2,128)}, u32[]{:S(2)}) copy-start(f32[1,1,8,16,4,2,128]{6,5,4,3,2,1,0:T(2,128)} %param.6) | copy-start | bytes 1572868
  2.2 1.0 %copy-start.2 = (bf16[384,512]{1,0:T(8,128)(2,1)S(1)}, bf16[384,512]{1,0:T(8,128)(2,1)}, u32[]{:S(2)}) copy-start(bf16[384,512]{1,0:T(8,128)(2,1)} %constant.4.clone.w_all) | copy-start | bytes 1179652
  3.2 0.9 %copy-start.3 = (f32[1,1,8,16,2,128]{5,4,3,2,1,0:T(2,128)S(1)}, f32[1,1,8,16,2,128]{5,4,3,2,1,0:T(2,128)}, u32[]{:S(2)}) copy-start(f32[1,1,8,16,2,128]{5,4,3,2,1,0:T(2,128)} %param.7) | copy-start | bytes 393220

commit v5 on v4

--- a/solution.py
+++ b/solution.py
@@ -100,8 +100,8 @@
     coeffs, phases, field_phases, w_all, w_last, out,
     cbuf, lpv, fpv, w_ref, wf_ref, cos1, sin1, cos_f, sin_f,
     send_a, recv_xa, send_ya, recv_ya, send_yb, recv_yb, recv_xb,
-    p1, phs, cos_t, sin_t, xs, res, s4, r1, gz, gy,
-    load_sem, x_send, x_recv, in_send, in_recv, s1_send, s1_recv, s2_send, s2_recv, ph_send, ph_recv,
+    p1, phs, cos_t, sin_t, xs, res, s4, r1, gz, gy, done,
+    load_sem, out_sem, x_send, x_recv, in_send, in_recv, s1_send, s1_recv, s2_send, s2_recv, ph_send, ph_recv,
 ):
     big_x = lax.axis_index("qx")
     big_y = lax.axis_index("qy")
@@ -421,14 +421,20 @@
                         box_h, box_v = n // 4, p * 8 + (a * 4 + n % 4)
                     rows = slice((a * 32 + n) * 8, (a * 32 + n + 1) * 8)
                     at = pl.ds(box_v * 2 + left, 1)
-                    out[box_h * 16 + box_v, left, k, pl.ds(half * 8, 8), :] = (
+                    done[c, k, box_h * 16 + box_v] = (
                         res[rows, 0:WIDE] * cos_f[k, box_h, at, :]
                         + res[rows, WIDE : 2 * WIDE] * sin_f[k, box_h, at, :]
                     )
             return carry
 
         lax.fori_loop(0, 2, piece, 0)
-
+        store = pltpu.make_async_copy(
+            done.at[c, k], out.at[:, left, k, pl.ds(half * 8, 8)], out_sem.at[c, k]
+        )
+        store.start()
+        stores.append(store)
+
+    stores = []
     rotate_first(0)
     pl.semaphore_wait(barrier, greeted)
     enter(0)
@@ -476,6 +482,8 @@
         for k in range(2):
             wait_for(r1.at[c, k, pl.ds(0, 31)], s1_send.at[c, k])
             wait_for(gz.at[c, pl.ds(0, 3)], s2_send.at[c, k])
+    for store in stores:
+        store.wait()
     wait_for(p1.at[pl.ds(0, 31)], ph_send.at[0])
     wait_for(phs.at[:, pl.ds(0, 3)], ph_send.at[1])
 
@@ -491,7 +499,7 @@
         butterfly_kernel,
         out_shape=jax.ShapeDtypeStruct((128, 2, 2, 16, WIDE), F32),
         in_specs=[pl.BlockSpec(memory_space=pltpu.HBM)] * 5,
-        out_specs=pl.BlockSpec(memory_space=pltpu.VMEM),
+        out_specs=pl.BlockSpec(memory_space=pltpu.HBM),
         scratch_shapes=[
             pltpu.VMEM((2, 128, 2, 16, WIDE), F32),
             vmem(128),
@@ -519,7 +527,9 @@
             vmem(4, 2, 32, 2),
             vmem(4, 4, 32),
             vmem(4, 4, 32),
+            vmem(4, 2, 128),
             dma((6,)),
+            dma((4, 2)),
             dma((4,)),
             dma((4,)),
             dma((4,)),
@@ -532,19 +542,51 @@
             dma((2,)),
         ],
         compiler_params=pltpu.CompilerParams(
-            collective_id=0, has_side_effects=True, vmem_limit_bytes=48 * 2**20
+            collective_id=0, has_side_effects=True, vmem_limit_bytes=60 * 2**20
         ),
         name="butterfly",
     )(coeffs, phases, field_phases, spread, last)
 
 
+def hand_on_kernel(done, out, held, in_sem, out_sem):
+    parts = in_sem.shape[0]
+    rows = done.shape[0] // parts
+    into, onto = [], []
+    for n in range(parts):
+        some = pl.ds(n * rows, rows)
+        into.append(pltpu.make_async_copy(done.at[some], held.at[some], in_sem.at[n]))
+        onto.append(pltpu.make_async_copy(held.at[some], out.at[some], out_sem.at[n]))
+        into[n].start()
+    for n in range(parts):
+        into[n].wait()
+        onto[n].start()
+    for n in range(parts):
+        onto[n].wait()
+
+
+def hand_on(done, parts=4):
+    return pl.pallas_call(
+        hand_on_kernel,
+        out_shape=jax.ShapeDtypeStruct(done.shape, F32),
+        in_specs=[pl.BlockSpec(memory_space=pltpu.HBM)],
+        out_specs=pl.BlockSpec(memory_space=pltpu.HBM),
+        scratch_shapes=[
+            pltpu.VMEM(done.shape, F32),
+            pltpu.SemaphoreType.DMA((parts,)),
+            pltpu.SemaphoreType.DMA((parts,)),
+        ],
+        compiler_params=pltpu.CompilerParams(vmem_limit_bytes=60 * 2**20),
+        name="hand_on",
+    )(done)
+
+
 def per_device(coeffs, level_phase, field_phase):
     spread, last = weights()
-    field = butterfly(
+    done = butterfly(
         coeffs.reshape(128, 2, 2, 16, WIDE), level_phase.reshape(128, 8, WIDE),
         field_phase.reshape(8, 32, WIDE), spread, last,
     )
-    return field.reshape(coeffs.shape)
+    return hand_on(done).reshape(coeffs.shape)
 
 
 def solution(mesh):

time: 84.2 us -> 81.5 us (0.968)
  local copies, waits for them, and re-layouts: 6.09 us -> 0 us
  Pallas kernels: 77.8 us -> 81.3 us
    unnamed x9 -> x0, local copies, waits for them, and re-layouts: 6.09 us -> none
    pallas_call x0 -> x1, Pallas kernels: none -> 3.3 us  [hand_on(): pl.pallas_call(hand_on_kernel, out_shape=jax.ShapeDtypeStruct(done.shape,...]
where the time goes in v5:
time: 81.5 us; the launch traced here: 81.3 us
  Pallas kernels  81.3 us (100%)
    pallas_call x1, Pallas kernels, butterfly(): pl.pallas_call(butterfly_kernel, out_shape=jax.ShapeDtypeStruct((128, 2,...  78 us
    pallas_call x1, Pallas kernels, hand_on(): pl.pallas_call(hand_on_kernel, out_shape=jax.ShapeDtypeStruct(done.shape,...  3.3 us

profile of v5, /device:TPU:1, one launch (start us, length us, event | category | flops | bytes accessed | tf_op | source)
XLA Modules:
  0.0 81.3 jit_solution(16378346808608695524)
XLA Ops:
  0.0 78.0 %butterfly.1.done = f32[128,2,2,16,128]{4,3,2,1,0:T(8,128)} custom-call(f32[128,2,2,16,128]{4,3,2,1,0:T(8,128)} %bitcast.4, f32[128,8,128]{2,1,0:T(8,128)} %bitcast.5, f32[8,32,128]{2,1,0:T(8,128)} %bitcast.6, bf16[384,512]{1,0:T(8,128)(2,1)} %constant.4.clone.w_all, bf16[4,384,256]{2,1,0:T(8,128)(2,1)} %constant.5.clone.w_last), custom_call_target="tpu_custom_call" | custom-call | tf_op jit(solution)/shard_map/butterfly/pallas_call | solution.py:498
  78.1 3.3 %hand_on.1 = f32[128,2,2,16,128]{4,3,2,1,0:T(8,128)} custom-call(f32[128,2,2,16,128]{4,3,2,1,0:T(8,128)} %butterfly.1.done), custom_call_target="tpu_custom_call" | custom-call | tf_op jit(solution)/shard_map/hand_on/pallas_call | solution.py:568

commit v6 on v5

--- a/solution.py
+++ b/solution.py
@@ -100,7 +100,7 @@
     coeffs, phases, field_phases, w_all, w_last, out,
     cbuf, lpv, fpv, w_ref, wf_ref, cos1, sin1, cos_f, sin_f,
     send_a, recv_xa, send_ya, recv_ya, send_yb, recv_yb, recv_xb,
-    p1, phs, cos_t, sin_t, xs, res, s4, r1, gz, gy, done,
+    pk, p1, pq, phs, cos_t, sin_t, xs, res, s4, r1, gz, gy, done,
     load_sem, out_sem, x_send, x_recv, in_send, in_recv, s1_send, s1_recv, s2_send, s2_recv, ph_send, ph_recv,
 ):
     big_x = lax.axis_index("qx")
@@ -231,28 +231,49 @@
             send_x(lambda t: recv_yb.at[h, :, t], recv_xb.at[h, x], x_send.at[c], x_recv.at[c])
             recv_xb[h, x] = recv_yb[h, :, x]
 
-    def send_phases():
-        send_in(lambda t: lpv.at[pl.ds(t * 4, 4)], p1.at[me_in], ph_send.at[0], ph_recv.at[0])
-        p1[me_in] = lpv[pl.ds(me_in * 4, 4)]
-
-    def pass_phases():
-        wait_for(p1.at[pl.ds(0, 31)], ph_recv.at[0])
-        send_x(lambda t: p1.at[:, t], phs.at[:, x], ph_send.at[1], ph_recv.at[1])
-        phs[:, x] = p1[:, x]
-
-    def phase_tables():
-        wait_for(phs.at[:, pl.ds(0, 3)], ph_recv.at[1])
-
-        def table(i, carry):
-            some = pl.ds(i * 8, 8)
-            angle = phs[pl.ds(i * 2, 2)].reshape(8, 8, WIDE)
-            cos, sin = turn_tables(angle, True)
-            for k in range(2):
-                cos_t[k, some] = cos[k]
-                sin_t[k, some] = sin[k]
-            return carry
-
-        lax.fori_loop(0, 16, table, 0)
+    spans = (pl.ds(0, 1), pl.ds(1, 2))
+
+    def pack_phases(j, carry):
+        for n in range(4):
+            i = j * 4 + n
+            for level in range(3):
+                for vx in range(4):
+                    pk[i, level, 2 * vx : 2 * vx + 2] = lpv[i * 4 + vx, 2 * level + 2 : 2 * level + 4]
+        return carry
+
+    def send_phases(part):
+        span = spans[part]
+        send_in(lambda t: pk.at[t, span], p1.at[me_in, span], ph_send.at[part], ph_recv.at[part])
+        p1[me_in, span] = pk[me_in, span]
+
+    def pass_phases(part):
+        span = spans[part]
+        wait_for(p1.at[pl.ds(0, 31), span], ph_recv.at[part])
+
+        def pack(i, carry):
+            for level in (0,) if part == 0 else (1, 2):
+                for sx in range(4):
+                    for sy in range(4):
+                        pq[sx, level, i, 2 * sy : 2 * sy + 2] = p1[i * 4 + sy, level, 2 * sx : 2 * sx + 2]
+            return carry
+
+        lax.fori_loop(0, 8, pack, 0)
+        send_x(lambda t: pq.at[t, span], phs.at[x, span], ph_send.at[2 + part], ph_recv.at[2 + part])
+        phs[x, span] = pq[x, span]
+
+    def phase_tables(part):
+        span = spans[part]
+        wait_for(phs.at[pl.ds(0, 3), span], ph_recv.at[2 + part])
+
+        def table(sx, carry):
+            for level in (0,) if part == 0 else (1, 2):
+                cos, sin = turn_tables(phs[sx, level], True)
+                for k in range(2):
+                    cos_t[level, k, sx] = cos[k]
+                    sin_t[level, k, sx] = sin[k]
+            return carry
+
+        lax.fori_loop(0, 4, table, 0)
 
     def field_tables():
         loads[4].wait()
@@ -274,20 +295,16 @@
         xs[rows, 2 * WIDE : 3 * WIDE] = high
 
     def multiply():
-        def piece(i, carry):
-            rows = pl.ds(pl.multiple_of(i * 256, 256), 256)
-            res[rows, :] = jnp.dot(xs[rows, :], w_ref[...], preferred_element_type=F32)
-            return carry
-
-        lax.fori_loop(0, 2, piece, 0)
-
-    def turned_sum(parts, row):
+        res[...] = jnp.dot(xs[...], w_ref[...], preferred_element_type=F32)
+
+    def turned_sum(parts, level, left):
         direct = None
         crossed = None
-        for block, column, k, place in parts:
+        for block, column, k, at_x, at_y, at_v in parts:
             value = res[pl.ds(pl.multiple_of(block * 8, 8), 8), column * WIDE : (column + 1) * WIDE]
-            d = value * cos_t[k, place, pl.ds(row, 1), :]
-            e = value * sin_t[k, place, pl.ds(row, 1), :]
+            row = pl.ds(2 * at_y + left, 1)
+            d = value * cos_t[level, k, at_v, at_x, row, :]
+            e = value * sin_t[level, k, at_v, at_x, row, :]
             direct = d if direct is None else direct + d
             crossed = e if crossed is None else crossed + e
         return direct + swap(crossed)
@@ -314,7 +331,7 @@
         lax.fori_loop(0, 4, first, 0)
         multiply()
 
-    def other_levels(c):
+    def level_two(c):
         left = c // 2
 
         def second(a, carry):
@@ -325,14 +342,16 @@
                     for x0 in range(2):
                         for y1 in range(2):
                             block = a * 16 + (x0 * 8 + y3 * 4 + y2 * 2 + y1)
-                            place = a * 32 + (x0 * 16 + y3 * 8 + y2 * 4 + y1 * 2 + y0)
-                            parts.append((block, k * 2 + y0, k, place))
-                    outs.append(turned_sum(parts, 2 + left))
+                            parts.append((block, k * 2 + y0, k, a * 2 + x0, y3 * 2 + y2, y1 * 2 + y0))
+                    outs.append(turned_sum(parts, 0, left))
                 put_parts(a * 128 + (y3 * 4 + y2 * 2 + y0) * 16, jnp.concatenate(outs, axis=0))
             return carry
 
         lax.fori_loop(0, 4, second, 0)
         multiply()
+
+    def other_levels(c):
+        left = c // 2
 
         def third(x2, carry):
             for y3, y0, k in DIGITS:
@@ -343,9 +362,9 @@
                         for x1 in range(2):
                             for y2 in range(2):
                                 block = x2 * 32 + (x1 * 16 + y3 * 8 + y2 * 4 + y0 * 2 + k)
-                                place = x2 * 64 + (x1 * 32 + x0 * 16 + y3 * 8 + y2 * 4 + y1 * 2 + y0)
-                                parts.append((block, x0 * 2 + y1, k, place))
-                        outs.append(turned_sum(parts, 4 + left))
+                                at_x = x2 * 4 + (x1 * 2 + x0)
+                                parts.append((block, x0 * 2 + y1, k, at_x, y3 * 2 + y2, y1 * 2 + y0))
+                        outs.append(turned_sum(parts, 1, left))
                     put_parts(
                         x2 * 256 + (y3 * 8 + y0 * 4 + k * 2 + x0) * 16, jnp.concatenate(outs, axis=0)
                     )
@@ -362,12 +381,12 @@
                         for x2 in range(2):
                             for y3 in range(2):
                                 block = y0 * 8 + (x2 * 32 + y3 * 16 + k * 4 + x0 * 2 + y1)
-                                place = y0 + (x2 * 64 + x1 * 32 + x0 * 16 + y3 * 8 + y2 * 4 + y1 * 2)
-                                parts.append((block, x1 * 2 + y2, k, place))
+                                at_x = x2 * 4 + x1 * 2 + x0
+                                parts.append((block, x1 * 2 + y2, k, at_x, y3 * 2 + y2, y1 * 2 + y0))
                         if k == 0:
-                            s4[c, 0, y0 + (x0 * 8 + y2 * 4 + y1 * 2), x1] = turned_sum(parts, 6 + left)
+                            s4[c, 0, y0 + (x0 * 8 + y2 * 4 + y1 * 2), x1] = turned_sum(parts, 2, left)
                         else:
-                            s4[c, 1, y0 + (x1 * 8 + x0 * 4 + y1 * 2), y2] = turned_sum(parts, 6 + left)
+                            s4[c, 1, y0 + (x1 * 8 + x0 * 4 + y1 * 2), y2] = turned_sum(parts, 2, left)
             return carry
 
         lax.fori_loop(0, 2, fourth, 0)
@@ -435,44 +454,52 @@
         stores.append(store)
 
     stores = []
+    lax.fori_loop(0, 8, pack_phases, 0)
     rotate_first(0)
     pl.semaphore_wait(barrier, greeted)
     enter(0)
-    send_phases()
+    send_phases(0)
+    send_phases(1)
     rotate_first(1)
     enter(1)
     rotate_first(2)
     enter(2)
+    pass_phases(0)
     pass_on(0)
-    pass_phases()
+    pass_phases(1)
     rotate_first(3)
     enter(3)
+    pass_on(2)
     pass_on(1)
-    pass_on(2)
     loads[3].wait()
     field_tables()
+    phase_tables(0)
     level_one(0)
-    phase_tables()
+    level_two(0)
+    phase_tables(1)
     other_levels(0)
+    pass_on(3)
+    level_one(2)
+    level_two(2)
+    other_levels(2)
     level_one(1)
-    pass_on(3)
-    other_levels(1)
     out_last(0, 0)
     out_last(0, 1)
-    level_one(2)
-    other_levels(2)
+    level_two(1)
+    other_levels(1)
+    out_last(2, 0)
     level_one(3)
+    level_two(3)
+    out_last(2, 1)
+    other_levels(3)
+    out_last(1, 1)
     out_last(1, 0)
-    out_last(1, 1)
-    other_levels(3)
-    out_last(2, 0)
-    out_last(2, 1)
     loads[5].wait()
     finish(0, 0)
     finish(0, 1)
+    out_last(3, 1)
     out_last(3, 0)
-    out_last(3, 1)
-    for c in range(1, 4):
+    for c in (2, 1, 3):
         finish(c, 0)
         finish(c, 1)
     for c in range(4):
@@ -484,8 +511,9 @@
             wait_for(gz.at[c, pl.ds(0, 3)], s2_send.at[c, k])
     for store in stores:
         store.wait()
-    wait_for(p1.at[pl.ds(0, 31)], ph_send.at[0])
-    wait_for(phs.at[:, pl.ds(0, 3)], ph_send.at[1])
+    for part in range(2):
+        wait_for(p1.at[pl.ds(0, 31), spans[part]], ph_send.at[part])
+        wait_for(phs.at[pl.ds(0, 3), spans[part]], ph_send.at[2 + part])
 
 
 def butterfly(coeffs, phases, field_phases, spread, last):
@@ -517,10 +545,12 @@
             vmem(2, 32, 4),
             vmem(2, 32, 4),
             vmem(2, 4, 32),
-            vmem(32, 4),
-            vmem(32, 4),
-            vmem(2, 128),
-            vmem(2, 128),
+            vmem(32, 3),
+            vmem(32, 3),
+            vmem(4, 3, 8),
+            vmem(4, 3, 8),
+            vmem(3, 2, 4, 8),
+            vmem(3, 2, 4, 8),
             pltpu.VMEM((512, 3 * WIDE), BF16),
             pltpu.VMEM((512, 4 * WIDE), F32),
             vmem(4, 2, 16, 2),
@@ -538,8 +568,8 @@
             dma((4, 2)),
             dma((4, 2)),
             dma((4, 2)),
-            dma((2,)),
-            dma((2,)),
+            dma((4,)),
+            dma((4,)),
         ],
         compiler_params=pltpu.CompilerParams(
             collective_id=0, has_side_effects=True, vmem_limit_bytes=60 * 2**20

time: 81.5 us -> 80.4 us (0.987)
  Pallas kernels: 81.3 us -> 80.2 us
    pallas_call x1, Pallas kernels: 78 us -> 76.9 us  [butterfly(): pl.pallas_call(butterfly_kernel, out_shape=jax.ShapeDtypeStruct((128, 2,...]
where the time goes in v6:
time: 80.4 us; the launch traced here: 80.3 us
  Pallas kernels  80.2 us (100%)
    pallas_call x1, Pallas kernels, butterfly(): pl.pallas_call(butterfly_kernel, out_shape=jax.ShapeDtypeStruct((128, 2,...  76.9 us
    pallas_call x1, Pallas kernels, hand_on(): pl.pallas_call(hand_on_kernel, out_shape=jax.ShapeDtypeStruct(done.shape,...  3.3 us

profile of v6, /device:TPU:1, one launch (start us, length us, event | category | flops | bytes accessed | tf_op | source)
XLA Modules:
  0.0 80.3 jit_solution(4593935710697542675)
XLA Ops:
  0.0 76.9 %butterfly.1.done = f32[128,2,2,16,128]{4,3,2,1,0:T(8,128)} custom-call(f32[128,2,2,16,128]{4,3,2,1,0:T(8,128)} %bitcast.4, f32[128,8,128]{2,1,0:T(8,128)} %bitcast.5, f32[8,32,128]{2,1,0:T(8,128)} %bitcast.6, bf16[384,512]{1,0:T(8,128)(2,1)} %constant.4.clone.w_all, bf16[4,384,256]{2,1,0:T(8,128)(2,1)} %constant.5.clone.w_last), custom_call_target="tpu_custom_call" | custom-call | tf_op jit(solution)/shard_map/butterfly/pallas_call | solution.py:526
  77.0 3.3 %hand_on.1 = f32[128,2,2,16,128]{4,3,2,1,0:T(8,128)} custom-call(f32[128,2,2,16,128]{4,3,2,1,0:T(8,128)} %butterfly.1.done), custom_call_target="tpu_custom_call" | custom-call | tf_op jit(solution)/shard_map/hand_on/pallas_call | solution.py:598

commit v7 on v6

--- a/solution.py
+++ b/solution.py
@@ -92,16 +92,59 @@
     return cos, sin
 
 
+def place_parts(xs, row, value):
+    high, low = split_parts(value)
+    rows = pl.ds(pl.multiple_of(row, 16), 16)
+    xs[rows, 0:WIDE] = high
+    xs[rows, WIDE : 2 * WIDE] = low
+    xs[rows, 2 * WIDE : 3 * WIDE] = high
+
+
+def last_stage(got, put, k, left, xs, res, wf_ref, cos_f, sin_f):
+    def piece(p, carry):
+        for a in range(2):
+            for n in range(16):
+                place_parts(xs, (a * 16 + n) * 16, got[p * 2 + a, pl.ds(2 * n, 2)].reshape(16, WIDE))
+        res[:, 0 : 2 * WIDE] = jnp.dot(xs[...], wf_ref[...], preferred_element_type=F32)
+        for a in range(2):
+            for n in range(32):
+                if k == 0:
+                    box_h, box_v = p * 4 + (a * 2 + n // 16), n % 16
+                else:
+                    box_h, box_v = n // 4, p * 8 + (a * 4 + n % 4)
+                rows = slice((a * 32 + n) * 8, (a * 32 + n + 1) * 8)
+                at = pl.ds(box_v * 2 + left, 1)
+                put(
+                    box_h * 16 + box_v,
+                    res[rows, 0:WIDE] * cos_f[k, box_h, at, :]
+                    + res[rows, WIDE : 2 * WIDE] * sin_f[k, box_h, at, :],
+                )
+        return carry
+
+    lax.fori_loop(0, 2, piece, 0)
+
+
+def field_turns(fpv, cos_f, sin_f):
+    def table(i, carry):
+        cos, sin = turn_tables(fpv[i], False)
+        for k in range(2):
+            cos_f[k, i] = cos[k]
+            sin_f[k, i] = sin[k]
+        return carry
+
+    lax.fori_loop(0, 8, table, 0)
+
+
 def wait_for(ref, sem):
     pltpu.make_async_copy(ref, ref, sem).wait()
 
 
 def butterfly_kernel(
-    coeffs, phases, field_phases, w_all, w_last, out,
+    coeffs, phases, field_phases, w_all, w_last, out, gz3, gy3,
     cbuf, lpv, fpv, w_ref, wf_ref, cos1, sin1, cos_f, sin_f,
     send_a, recv_xa, send_ya, recv_ya, send_yb, recv_yb, recv_xb,
     pk, p1, pq, phs, cos_t, sin_t, xs, res, s4, r1, gz, gy, done,
-    load_sem, out_sem, x_send, x_recv, in_send, in_recv, s1_send, s1_recv, s2_send, s2_recv, ph_send, ph_recv,
+    load_sem, out_sem, own_sem, x_send, x_recv, in_send, in_recv, s1_send, s1_recv, s2_send, s2_recv, ph_send, ph_recv,
 ):
     big_x = lax.axis_index("qx")
     big_y = lax.axis_index("qy")
@@ -277,22 +320,10 @@
 
     def field_tables():
         loads[4].wait()
-
-        def table(i, carry):
-            cos, sin = turn_tables(fpv[i], False)
-            for k in range(2):
-                cos_f[k, i] = cos[k]
-                sin_f[k, i] = sin[k]
-            return carry
-
-        lax.fori_loop(0, 8, table, 0)
+        field_turns(fpv, cos_f, sin_f)
 
     def put_parts(row, value):
-        high, low = split_parts(value)
-        rows = pl.ds(pl.multiple_of(row, 16), 16)
-        xs[rows, 0:WIDE] = high
-        xs[rows, WIDE : 2 * WIDE] = low
-        xs[rows, 2 * WIDE : 3 * WIDE] = high
+        place_parts(xs, row, value)
 
     def multiply():
         res[...] = jnp.dot(xs[...], w_ref[...], preferred_element_type=F32)
@@ -406,18 +437,26 @@
 
     def out_last(c, k):
         wait_for(r1.at[c, k, pl.ds(0, 31)], s1_recv.at[c, k])
+        to_z, to_y = (gz3, gy3) if c == 3 else (gz.at[c], gy.at[c])
         for d in (2, 1, 3):
             if k == 0:
                 send(
-                    r1.at[c, 0, :, z_odd[d]], gz.at[c, z], s2_send.at[c, 0], s2_recv.at[c, 0],
+                    r1.at[c, 0, :, z_odd[d]], to_z.at[z], s2_send.at[c, 0], s2_recv.at[c, 0],
                     (dev_x[d][0], big_y),
                 )
             else:
                 send(
-                    r1.at[c, 1, :, y_odd[d]], gy.at[c, y], s2_send.at[c, 1], s2_recv.at[c, 1],
+                    r1.at[c, 1, :, y_odd[d]], to_y.at[y], s2_send.at[c, 1], s2_recv.at[c, 1],
                     (big_x, dev_y[d][0]),
                 )
-        if k == 0:
+        if c == 3:
+            kept.append(
+                pltpu.make_async_copy(r1.at[c, 0, :, z_odd[0]], gz3.at[z], own_sem.at[0])
+                if k == 0
+                else pltpu.make_async_copy(r1.at[c, 1, :, y_odd[0]], gy3.at[y], own_sem.at[1])
+            )
+            kept[-1].start()
+        elif k == 0:
             gz[c, z] = r1[c, 0, :, z_odd[0]]
         else:
             gy[c, y] = r1[c, 1, :, y_odd[0]]
@@ -427,26 +466,10 @@
         got = gz if k == 0 else gy
         wait_for(got.at[c, pl.ds(0, 3)], s2_recv.at[c, k])
 
-        def piece(p, carry):
-            for a in range(2):
-                for n in range(16):
-                    put_parts((a * 16 + n) * 16, got[c, p * 2 + a, pl.ds(2 * n, 2)].reshape(16, WIDE))
-            res[:, 0 : 2 * WIDE] = jnp.dot(xs[...], wf_ref[...], preferred_element_type=F32)
-            for a in range(2):
-                for n in range(32):
-                    if k == 0:
-                        box_h, box_v = p * 4 + (a * 2 + n // 16), n % 16
-                    else:
-                        box_h, box_v = n // 4, p * 8 + (a * 4 + n % 4)
-                    rows = slice((a * 32 + n) * 8, (a * 32 + n + 1) * 8)
-                    at = pl.ds(box_v * 2 + left, 1)
-                    done[c, k, box_h * 16 + box_v] = (
-                        res[rows, 0:WIDE] * cos_f[k, box_h, at, :]
-                        + res[rows, WIDE : 2 * WIDE] * sin_f[k, box_h, at, :]
-                    )
-            return carry
-
-        lax.fori_loop(0, 2, piece, 0)
+        def put(place, value):
+            done[c, k, place] = value
+
+        last_stage(got.at[c], put, k, left, xs, res, wf_ref, cos_f, sin_f)
         store = pltpu.make_async_copy(
             done.at[c, k], out.at[:, left, k, pl.ds(half * 8, 8)], out_sem.at[c, k]
         )
@@ -454,62 +477,66 @@
         stores.append(store)
 
     stores = []
+    kept = []
     lax.fori_loop(0, 8, pack_phases, 0)
     rotate_first(0)
     pl.semaphore_wait(barrier, greeted)
     enter(0)
     send_phases(0)
     send_phases(1)
+    rotate_first(2)
+    enter(2)
     rotate_first(1)
     enter(1)
-    rotate_first(2)
-    enter(2)
     pass_phases(0)
+    pass_phases(1)
     pass_on(0)
-    pass_phases(1)
+    pass_on(2)
+    pass_on(1)
     rotate_first(3)
     enter(3)
-    pass_on(2)
-    pass_on(1)
     loads[3].wait()
     field_tables()
+    level_one(0)
     phase_tables(0)
-    level_one(0)
     level_two(0)
     phase_tables(1)
     other_levels(0)
+    level_one(1)
+    level_two(1)
+    other_levels(1)
+    out_last(0, 0)
     pass_on(3)
     level_one(2)
+    out_last(0, 1)
+    out_last(1, 0)
+    out_last(1, 1)
     level_two(2)
     other_levels(2)
-    level_one(1)
-    out_last(0, 0)
-    out_last(0, 1)
-    level_two(1)
-    other_levels(1)
-    out_last(2, 0)
     level_one(3)
     level_two(3)
+    other_levels(3)
+    out_last(2, 0)
     out_last(2, 1)
-    other_levels(3)
-    out_last(1, 1)
-    out_last(1, 0)
     loads[5].wait()
     finish(0, 0)
+    out_last(3, 1)
+    finish(1, 0)
+    out_last(3, 0)
     finish(0, 1)
-    out_last(3, 1)
-    out_last(3, 0)
-    for c in (2, 1, 3):
-        finish(c, 0)
-        finish(c, 1)
+    finish(1, 1)
+    finish(2, 0)
+    finish(2, 1)
+    wait_for(gz3.at[pl.ds(0, 3)], s2_recv.at[3, 0])
+    wait_for(gy3.at[pl.ds(0, 3)], s2_recv.at[3, 1])
     for c in range(4):
         h = c % 2
         wait_for(recv_xa.at[h, pl.ds(0, 3)], x_send.at[c])
         wait_for((recv_ya if c < 2 else recv_yb).at[h, pl.ds(0, 31)], in_send.at[c])
         for k in range(2):
             wait_for(r1.at[c, k, pl.ds(0, 31)], s1_send.at[c, k])
-            wait_for(gz.at[c, pl.ds(0, 3)], s2_send.at[c, k])
-    for store in stores:
+            wait_for(gz.at[0, pl.ds(0, 3)], s2_send.at[c, k])
+    for store in stores + kept:
         store.wait()
     for part in range(2):
         wait_for(p1.at[pl.ds(0, 31), spans[part]], ph_send.at[part])
@@ -525,9 +552,13 @@
 
     return pl.pallas_call(
         butterfly_kernel,
-        out_shape=jax.ShapeDtypeStruct((128, 2, 2, 16, WIDE), F32),
+        out_shape=(
+            jax.ShapeDtypeStruct((128, 2, 2, 16, WIDE), F32),
+            jax.ShapeDtypeStruct((4, 32) + tile, F32),
+            jax.ShapeDtypeStruct((4, 32) + tile, F32),
+        ),
         in_specs=[pl.BlockSpec(memory_space=pltpu.HBM)] * 5,
-        out_specs=pl.BlockSpec(memory_space=pltpu.HBM),
+        out_specs=tuple(pl.BlockSpec(memory_space=pltpu.HBM) for _ in range(3)),
         scratch_shapes=[
             pltpu.VMEM((2, 128, 2, 16, WIDE), F32),
             vmem(128),
@@ -555,11 +586,12 @@
             pltpu.VMEM((512, 4 * WIDE), F32),
             vmem(4, 2, 16, 2),
             vmem(4, 2, 32, 2),
-            vmem(4, 4, 32),
-            vmem(4, 4, 32),
-            vmem(4, 2, 128),
+            vmem(3, 4, 32),
+            vmem(3, 4, 32),
+            vmem(3, 2, 128),
             dma((6,)),
-            dma((4, 2)),
+            dma((3, 2)),
+            dma((2,)),
             dma((4,)),
             dma((4,)),
             dma((4,)),
@@ -578,45 +610,81 @@
     )(coeffs, phases, field_phases, spread, last)
 
 
-def hand_on_kernel(done, out, held, in_sem, out_sem):
-    parts = in_sem.shape[0]
-    rows = done.shape[0] // parts
-    into, onto = [], []
-    for n in range(parts):
-        some = pl.ds(n * rows, rows)
-        into.append(pltpu.make_async_copy(done.at[some], held.at[some], in_sem.at[n]))
-        onto.append(pltpu.make_async_copy(held.at[some], out.at[some], out_sem.at[n]))
-        into[n].start()
-    for n in range(parts):
-        into[n].wait()
-        onto[n].start()
-    for n in range(parts):
-        onto[n].wait()
-
-
-def hand_on(done, parts=4):
+def complete_kernel(
+    done, gz3, gy3, field_phases, w_last, out, held, gzv, gyv, fpv, wf_ref, cos_f, sin_f, xs, res, in_sem, out_sem
+):
+    pick = (lax.axis_index("qx") // 4) * 2 + lax.axis_index("qy") // 8
+    half = held.shape[0] // 2
+    first, second = pl.ds(0, half), pl.ds(half, half)
+    upper, lower = pl.ds(0, 8), pl.ds(8, 8)
+    loads = [
+        pltpu.make_async_copy(src, dst, in_sem.at[n])
+        for n, (src, dst) in enumerate(
+            [(field_phases, fpv), (w_last.at[pick], wf_ref), (gz3, gzv), (gy3, gyv)]
+        )
+    ]
+    finished = [(first, 0), (second, 0), (slice(None), 1, slice(None), upper)]
+    into = [
+        pltpu.make_async_copy(done.at[part], held.at[part], in_sem.at[4 + n])
+        for n, part in enumerate(finished)
+    ]
+    for copy in loads + into:
+        copy.start()
+    parts = finished + [(slice(None), 1, k, lower) for k in range(2)]
+    onto = [
+        pltpu.make_async_copy(held.at[part], out.at[part], out_sem.at[n]) for n, part in enumerate(parts)
+    ]
+
+    loads[0].wait()
+    field_turns(fpv, cos_f, sin_f)
+    loads[1].wait()
+    for k, got in enumerate((gzv, gyv)):
+        loads[2 + k].wait()
+
+        def put(place, value, k=k):
+            held[place, 1, k, 8:16, :] = value
+
+        last_stage(got, put, k, 1, xs, res, wf_ref, cos_f, sin_f)
+        onto[3 + k].start()
+        if k == 0:
+            for n in range(3):
+                into[n].wait()
+                onto[n].start()
+    for copy in onto:
+        copy.wait()
+
+
+def complete(done, gz3, gy3, field_phases, last):
     return pl.pallas_call(
-        hand_on_kernel,
+        complete_kernel,
         out_shape=jax.ShapeDtypeStruct(done.shape, F32),
-        in_specs=[pl.BlockSpec(memory_space=pltpu.HBM)],
+        in_specs=[pl.BlockSpec(memory_space=pltpu.HBM)] * 5,
         out_specs=pl.BlockSpec(memory_space=pltpu.HBM),
         scratch_shapes=[
             pltpu.VMEM(done.shape, F32),
-            pltpu.SemaphoreType.DMA((parts,)),
-            pltpu.SemaphoreType.DMA((parts,)),
+            pltpu.VMEM((4, 32, 8, WIDE), F32),
+            pltpu.VMEM((4, 32, 8, WIDE), F32),
+            pltpu.VMEM((8, 32, WIDE), F32),
+            pltpu.VMEM((3 * WIDE, 2 * WIDE), BF16),
+            pltpu.VMEM((2, 8, 32, WIDE), F32),
+            pltpu.VMEM((2, 8, 32, WIDE), F32),
+            pltpu.VMEM((512, 3 * WIDE), BF16),
+            pltpu.VMEM((512, 2 * WIDE), F32),
+            pltpu.SemaphoreType.DMA((7,)),
+            pltpu.SemaphoreType.DMA((5,)),
         ],
         compiler_params=pltpu.CompilerParams(vmem_limit_bytes=60 * 2**20),
-        name="hand_on",
-    )(done)
+        name="complete",
+    )(done, gz3, gy3, field_phases, last)
 
 
 def per_device(coeffs, level_phase, field_phase):
     spread, last = weights()
-    done = butterfly(
-        coeffs.reshape(128, 2, 2, 16, WIDE), level_phase.reshape(128, 8, WIDE),
-        field_phase.reshape(8, 32, WIDE), spread, last,
+    angles = field_phase.reshape(8, 32, WIDE)
+    done, gz3, gy3 = butterfly(
+        coeffs.reshape(128, 2, 2, 16, WIDE), level_phase.reshape(128, 8, WIDE), angles, spread, last
     )
-    return hand_on(done).reshape(coeffs.shape)
+    return complete(done, gz3, gy3, angles, last).reshape(coeffs.shape)
 
 
 def solution(mesh):

time: 80.4 us -> 78 us (0.970)
  Pallas kernels: 80.2 us -> 77.8 us
    pallas_call x2, Pallas kernels: 80.2 us -> 77.8 us  [the longest x1 73.5 us: butterfly(): pl.pallas_call(butterfly_kernel, out_shape=(jax.ShapeDtypeStruct((128, 2,...]
where the time goes in v7:
time: 78 us; the launch traced here: 77.9 us
  Pallas kernels  77.8 us (100%)
    pallas_call x1, Pallas kernels, butterfly(): pl.pallas_call(butterfly_kernel, out_shape=(jax.ShapeDtypeStruct((128, 2,...  73.5 us
    pallas_call x1, Pallas kernels, complete(): pl.pallas_call(complete_kernel, out_shape=jax.ShapeDtypeStruct(done.shape...  4.36 us

profile of v7, /device:TPU:1, one launch (start us, length us, event | category | flops | bytes accessed | tf_op | source)
XLA Modules:
  0.0 77.9 jit_solution(104718748098761851)
XLA Ops:
  0.0 73.5 %butterfly.1 = (f32[128,2,2,16,128]{4,3,2,1,0:T(8,128)}, f32[4,32,8,128]{3,2,1,0:T(8,128)}, f32[4,32,8,128]{3,2,1,0:T(8,128)}) custom-call(f32[128,2,2,16,128]{4,3,2,1,0:T(8,128)} %bitcast.4, f32[128,8,128]{2,1,0:T(8,128)} %bitcast.7, f32[8,32,128]{2,1,0:T(8,128)} %bitcast.5, bf16[384,512]{1,0:T(8,128)(2,1)} %constant.4.clone.w_all, ...), custom_call_target="tpu_custom_call" | custom-call | tf_op jit(solution)/shard_map/butterfly/pallas_call | solution.py:553
  73.5 4.4 %complete.1 = f32[128,2,2,16,128]{4,3,2,1,0:T(8,128)} custom-call(f32[128,2,2,16,128]{4,3,2,1,0:T(8,128)} %get-tuple-element.8.done, f32[4,32,8,128]{3,2,1,0:T(8,128)} %get-tuple-element.9.gz3, f32[4,32,8,128]{3,2,1,0:T(8,128)} %get-tuple-element.10.gy3, f32[8,32,128]{2,1,0:T(8,128)} %bitcast.6, bf16[4,384,256]{2,1,0:T(8,128)(2,1)} %constant.5.clone.w_last), custom_call_target="tpu_custom_call" | custom-call | tf_op jit(solution)/shard_map/complete/pallas_call | solution.py:658

commit v8 on v7

--- a/solution.py
+++ b/solution.py
@@ -242,7 +242,7 @@
             send(src(xs_[dx]), dst, send_sem, recv_sem, (big_x, dev_y[0][dx]))
 
     def send_in(src, dst, send_sem, recv_sem):
-        for d in range(1, 32):
+        for d in range(31, 0, -1):
             there_x = dev_x[d // 8][(d // 4) % 2]
             send(src(there_x * 4 + ys[d % 4]), dst, send_sem, recv_sem, (there_x, dev_y[d % 4][0]))
 
@@ -422,7 +422,7 @@
 
         lax.fori_loop(0, 2, fourth, 0)
 
-        for d in range(1, 32):
+        for d in range(31, 0, -1):
             dc, dt, dx = d // 16, (d // 4) % 4, d % 4
             send(
                 s4.at[c, 0, cs[dc] * 8 + y_odd[dt] * 4 + xs_[dx]], r1.at[c, 0, me_z],
@@ -438,7 +438,7 @@
     def out_last(c, k):
         wait_for(r1.at[c, k, pl.ds(0, 31)], s1_recv.at[c, k])
         to_z, to_y = (gz3, gy3) if c == 3 else (gz.at[c], gy.at[c])
-        for d in (2, 1, 3):
+        for d in (1, 3, 2):
             if k == 0:
                 send(
                     r1.at[c, 0, :, z_odd[d]], to_z.at[z], s2_send.at[c, 0], s2_recv.at[c, 0],

time: 78 us -> 77.3 us (level)
  no operation moved by 1% of the time
where the time goes in v8:
time: 77.3 us; the launch traced here: 77.2 us
  Pallas kernels  77.2 us (100%)
    pallas_call x1, Pallas kernels, butterfly(): pl.pallas_call(butterfly_kernel, out_shape=(jax.ShapeDtypeStruct((128, 2,...  72.8 us
    pallas_call x1, Pallas kernels, complete(): pl.pallas_call(complete_kernel, out_shape=jax.ShapeDtypeStruct(done.shape...  4.36 us

profile of v8, /device:TPU:1, one launch (start us, length us, event | category | flops | bytes accessed | tf_op | source)
XLA Modules:
  0.0 77.2 jit_solution(13552545417449119583)
XLA Ops:
  0.0 72.8 %butterfly.1 = (f32[128,2,2,16,128]{4,3,2,1,0:T(8,128)}, f32[4,32,8,128]{3,2,1,0:T(8,128)}, f32[4,32,8,128]{3,2,1,0:T(8,128)}) custom-call(f32[128,2,2,16,128]{4,3,2,1,0:T(8,128)} %bitcast.4, f32[128,8,128]{2,1,0:T(8,128)} %bitcast.7, f32[8,32,128]{2,1,0:T(8,128)} %bitcast.5, bf16[384,512]{1,0:T(8,128)(2,1)} %constant.4.clone.w_all, ...), custom_call_target="tpu_custom_call" | custom-call | tf_op jit(solution)/shard_map/butterfly/pallas_call | solution.py:553
  72.8 4.4 %complete.1 = f32[128,2,2,16,128]{4,3,2,1,0:T(8,128)} custom-call(f32[128,2,2,16,128]{4,3,2,1,0:T(8,128)} %get-tuple-element.8.done, f32[4,32,8,128]{3,2,1,0:T(8,128)} %get-tuple-element.9.gz3, f32[4,32,8,128]{3,2,1,0:T(8,128)} %get-tuple-element.10.gy3, f32[8,32,128]{2,1,0:T(8,128)} %bitcast.6, bf16[4,384,256]{2,1,0:T(8,128)(2,1)} %constant.5.clone.w_last), custom_call_target="tpu_custom_call" | custom-call | tf_op jit(solution)/shard_map/complete/pallas_call | solution.py:658
